TPU v7x, 256 devices: a whole 4x4x8 slice. The times are simulated.
256 devices in a mesh: ctx: 32 (over z_lo, x, core), tp: 8 (over y, z_hi).
Axes of the slice: x: 4, y: 4, z: 8 (z_hi: 2, z_lo: 4; z = z_hi * 4 + z_lo), core: 2. Of those that a mesh axis runs over, the one named last changes fastest.
Arguments:
- out_cotangent: bfloat16 [4096, 8192], P('tp', 'ctx'), may hold values from -4 to 4
- query_rows: bfloat16 [4096, 8192], P('tp', 'ctx'), may hold values from -6 to 6
- key_rows: bfloat16 [4096, 8192], P('tp', 'ctx'), may hold values from -6 to 6
- value_rows: bfloat16 [4096, 8192], P('tp', 'ctx'), may hold values from -6 to 6
- long_filter: float32 [4096, 8192], P('tp', 'ctx'), may hold values from -0.0625 to 0.0625
- short_filter: float32 [3, 4096, 7], P(None, 'tp'), may hold values from -3 to 3
- out_weight: bfloat16 [4096, 4096], P(None, 'tp'), may hold values from -0.09375 to 0.09375
Outputs:
- feature_grad: bfloat16 [3, 4096, 8192], P(None, 'tp', 'ctx')
- filter_grad: float32 [4096, 8192], P('tp', 'ctx')
- out_weight_grad: float32 [4096, 4096], P('ctx', 'tp')
All inputs are finite; a program needn't handle non-finite values.
Results may differ from a plain program's by a relative error of at most 0.03.
Values may be sent and summed in bfloat16 or wider, within the bound.
No kernel may reach another device: no remote copies, remote signals or barrier semaphores. Data moves between devices by JAX's collectives and lax.ppermute only.
A program may use at most 64 MiB of HBM per device.

v0:
```python
import math

import jax
import jax.numpy as jnp
from jax import lax
from jax.sharding import PartitionSpec as P

DFT_PRECISION = lax.Precision.HIGH


def passed_along(value, axis, steps):
    count = lax.axis_size(axis)
    first, last = (max(0, -steps), min(count, count - steps))
    return lax.ppermute(value, axis, [(source, source + steps) for source in range(first, last)])


def dft_tables(total):
    first = 128
    second = total // first
    first_idx = jnp.arange(first, dtype=jnp.int32)
    second_idx = jnp.arange(second, dtype=jnp.int32)
    angle_one = (first_idx[:, None] * first_idx[None, :] % first).astype(jnp.float32) * (
        2.0 * math.pi / first
    )
    angle_two = (second_idx[:, None] * second_idx[None, :] % second).astype(jnp.float32) * (
        2.0 * math.pi / second
    )
    angle_tw = (first_idx[:, None] * second_idx[None, :] % total).astype(jnp.float32) * (
        2.0 * math.pi / total
    )
    return (
        jnp.cos(angle_one),
        jnp.sin(angle_one),
        jnp.cos(angle_two),
        jnp.sin(angle_two),
        jnp.cos(angle_tw),
        jnp.sin(angle_tw),
    )


def forward_dft(signal, tables):
    cos_one, sin_one, cos_two, sin_two, cos_tw, sin_tw = tables
    chans = signal.shape[0]
    grid = signal.reshape(chans, cos_one.shape[0], cos_two.shape[0])
    real_a = jnp.einsum("kt,cts->cks", cos_one, grid, precision=DFT_PRECISION)
    imag_a = -jnp.einsum("kt,cts->cks", sin_one, grid, precision=DFT_PRECISION)
    real_b = real_a * cos_tw + imag_a * sin_tw
    imag_b = imag_a * cos_tw - real_a * sin_tw
    real_out = jnp.einsum("cks,sm->ckm", real_b, cos_two, precision=DFT_PRECISION) + jnp.einsum(
        "cks,sm->ckm", imag_b, sin_two, precision=DFT_PRECISION
    )
    imag_out = jnp.einsum("cks,sm->ckm", imag_b, cos_two, precision=DFT_PRECISION) - jnp.einsum(
        "cks,sm->ckm", real_b, sin_two, precision=DFT_PRECISION
    )
    return (real_out, imag_out)


def inverse_dft(real_in, imag_in, tables, keep):
    cos_one, sin_one, cos_two, sin_two, cos_tw, sin_tw = tables
    chans = real_in.shape[0]
    total = cos_one.shape[0] * cos_two.shape[0]
    real_c = jnp.einsum("ckm,ms->cks", real_in, cos_two, precision=DFT_PRECISION) - jnp.einsum(
        "ckm,ms->cks", imag_in, sin_two, precision=DFT_PRECISION
    )
    imag_c = jnp.einsum("ckm,ms->cks", imag_in, cos_two, precision=DFT_PRECISION) + jnp.einsum(
        "ckm,ms->cks", real_in, sin_two, precision=DFT_PRECISION
    )
    real_d = real_c * cos_tw - imag_c * sin_tw
    imag_d = imag_c * cos_tw + real_c * sin_tw
    signal = jnp.einsum("tk,cks->cts", cos_one, real_d, precision=DFT_PRECISION) - jnp.einsum(
        "tk,cks->cts", sin_one, imag_d, precision=DFT_PRECISION
    )
    return (signal.reshape(chans, total) / total)[:, :keep]


def channel_work(kv_cols, gated_cols, filter_cols):
    length = kv_cols.shape[1]
    tables = dft_tables(2 * length)

    def padded(values):
        return jnp.pad(values.astype(jnp.float32), ((0, 0), (0, length)))

    kv_real, kv_imag = forward_dft(padded(kv_cols), tables)
    gated_real, gated_imag = forward_dft(padded(gated_cols), tables)
    filter_real, filter_imag = forward_dft(padded(filter_cols), tables)
    conv_cols = inverse_dft(
        filter_real * kv_real - filter_imag * kv_imag,
        filter_real * kv_imag + filter_imag * kv_real,
        tables,
        length,
    )
    adjoint_cols = inverse_dft(
        filter_real * gated_real + filter_imag * gated_imag,
        filter_real * gated_imag - filter_imag * gated_real,
        tables,
        length,
    )
    corr_cols = inverse_dft(
        gated_real * kv_real + gated_imag * kv_imag,
        gated_imag * kv_real - gated_real * kv_imag,
        tables,
        length,
    )
    return (conv_cols.astype(jnp.bfloat16), adjoint_cols.astype(jnp.bfloat16), corr_cols)


def local(out_cotangent, query_rows, key_rows, value_rows, long_filter, short_filter, out_weight):
    gathered = lax.all_gather(out_cotangent, "tp", axis=0, tiled=True)
    inner_grad = lax.dot_general(
        out_weight, gathered, (((0,), (0,)), ((), ())), preferred_element_type=jnp.float32
    ).astype(jnp.bfloat16)
    query_wide = query_rows.astype(jnp.float32)
    kv_product = (key_rows.astype(jnp.float32) * value_rows.astype(jnp.float32)).astype(
        jnp.bfloat16
    )
    gated = (inner_grad.astype(jnp.float32) * query_wide).astype(jnp.bfloat16)
    kv_cols, gated_cols = (
        lax.all_to_all(kv_product, "ctx", split_axis=0, concat_axis=1, tiled=True),
        lax.all_to_all(gated, "ctx", split_axis=0, concat_axis=1, tiled=True),
    )
    filter_cols = lax.all_to_all(long_filter, "ctx", split_axis=0, concat_axis=1, tiled=True)
    conv_cols, adjoint_cols, corr_cols = channel_work(kv_cols, gated_cols, filter_cols)
    conv_out, kv_grad = (
        lax.all_to_all(conv_cols, "ctx", split_axis=1, concat_axis=0, tiled=True),
        lax.all_to_all(adjoint_cols, "ctx", split_axis=1, concat_axis=0, tiled=True),
    )
    filter_grad = lax.all_to_all(
        corr_cols.astype(jnp.bfloat16), "ctx", split_axis=1, concat_axis=0, tiled=True
    ).astype(corr_cols.dtype)
    conv_wide = conv_out.astype(jnp.float32)
    mixed_inner = (query_wide * conv_wide).astype(jnp.bfloat16)
    kv_wide = kv_grad.astype(jnp.float32)
    q_grad = (inner_grad.astype(jnp.float32) * conv_wide).astype(jnp.bfloat16)
    k_grad = (kv_wide * value_rows.astype(jnp.float32)).astype(jnp.bfloat16)
    v_grad = (kv_wide * key_rows.astype(jnp.float32)).astype(jnp.bfloat16)
    post_grad = jnp.stack([q_grad, k_grad, v_grad])
    taps = short_filter.shape[2]
    local_len = post_grad.shape[2]
    following = passed_along(post_grad[:, :, : taps - 1], "ctx", -1)
    extended = jnp.concatenate([post_grad, following], axis=2).astype(jnp.float32)
    summed = jnp.zeros(post_grad.shape, jnp.float32)
    for offset in range(taps):
        summed = (
            summed
            + short_filter[:, :, offset][:, :, None] * extended[:, :, offset : offset + local_len]
        )
    feature_grad = summed.astype(jnp.bfloat16)
    out_weight_grad = lax.psum_scatter(
        lax.dot_general(
            gathered, mixed_inner, (((1,), (1,)), ((), ())), preferred_element_type=jnp.float32
        ).astype(jnp.bfloat16),
        "ctx",
        scatter_dimension=0,
        tiled=True,
    ).astype(jnp.float32)
    return (feature_grad, filter_grad, out_weight_grad)


def solution(mesh):
    return jax.shard_map(
        local,
        mesh=mesh,
        in_specs=(
            P("tp", "ctx"),
            P("tp", "ctx"),
            P("tp", "ctx"),
            P("tp", "ctx"),
            P("tp", "ctx"),
            P(None, "tp", None),
            P(None, "tp"),
        ),
        out_specs=(P(None, "tp", "ctx"), P("tp", "ctx"), P("ctx", "tp")),
        check_vma=False,
    )
```

profile of v0, /device:TPU:8, one launch (start us, length us, event | category | flops | bytes accessed | tf_op | source)
XLA Modules:
  0.0 330.7 jit_solution(13719932864679443705)
XLA Ops:
  7.2 1.1 copy.151
  8.3 1.1 copy.152
  9.5 0.8 copy.153
  10.3 8.8 %all-to-all-start.1 = ((bf16[32,16,256]{2,1,0:T(8,128)(2,1)}), bf16[32,16,256]{2,1,0:T(8,128)(2,1)S(1)}, u32[]{:S(2)}, u32[]{:S(2)}) async-start(bf16[32,16,256]{2,1,0:T(8,128)(2,1)} %bitcast.6), calls=%async_computation.1 | async-start | bytes 524288 | tf_op jit(solution)/shard_map/all_to_all | solution.py:118
  20.7 9.5 %all-to-all-done.1 = bf16[32,16,256]{2,1,0:T(8,128)(2,1)S(1)} async-done(((bf16[32,16,256]{2,1,0:T(8,128)(2,1)}), bf16[32,16,256]{2,1,0:T(8,128)(2,1)S(1)}, u32[]{:S(2)}, u32[]{:S(2)}) %all-to-all-start.1) | async-done | bytes 262176 | tf_op jit(solution)/shard_map/all_to_all | solution.py:118
  30.2 4.4 %all-to-all-start = ((f32[32,16,256]{2,1,0:T(8,128)}), f32[32,16,256]{2,1,0:T(8,128)S(1)}, u32[]{:S(2)}, u32[]{:S(2)}) async-start(f32[32,16,256]{2,1,0:T(8,128)} %bitcast), calls=%async_computation | async-start | bytes 1048576 | tf_op jit(solution)/shard_map/all_to_all | solution.py:121
  35.5 0.7 fusion.9
  36.3 1.2 fusion.62
  37.5 1.2 fusion.61
  38.7 2.2 convolution_subtract_fusion.7
  40.8 2.2 convolution_add_fusion.4
  43.0 12.6 %all-to-all-done = f32[32,16,256]{2,1,0:T(8,128)S(1)} async-done(((f32[32,16,256]{2,1,0:T(8,128)}), f32[32,16,256]{2,1,0:T(8,128)S(1)}, u32[]{:S(2)}, u32[]{:S(2)}) %all-to-all-start) | async-done | bytes 524320 | tf_op jit(solution)/shard_map/all_to_all | solution.py:121
  55.9 1.1 fusion.13
  57.0 1.1 convolution_bitcast_fusion.2
  58.2 1.2 fusion.60
  59.4 2.2 convolution_subtract_fusion.8
  61.6 41.9 %all-gather.2.cloned.1.call-done = bf16[4096,256]{1,0:T(8,128)(2,1)} async-done(((bf16[512,256]{1,0:T(8,128)(2,1)}), bf16[4096,256]{1,0:T(8,128)(2,1)}) %all-gather.2.cloned.1.call-update) | async-done | bytes 2097168 | tf_op jit(solution)/shard_map/all_gather | solution.py:108
  103.5 5.2 %fusion.45 = (bf16[512,256]{0,1:T(8,128)(2,1)S(1)}, f32[512,256]{0,1:T(8,128)}) fusion(bf16[512,256]{0,1:T(8,128)(2,1)S(1)} %copy.170, bf16[4096,512]{1,0:T(8,128)(2,1)} %param.13, bf16[4096,256]{1,0:T(8,128)(2,1)} %all-gather.2.cloned.1.call-done), kind=kOutput, calls=%fused_computation.94 | convolution fusion | flops 1074397184 | bytes 7340032 | tf_op jit(solution)/shard_map/dot_general | solution.py:109
  108.7 0.8 copy.171
  109.5 4.6 %all-to-all-start.3 = ((bf16[32,16,256]{2,1,0:T(8,128)(2,1)}), bf16[32,16,256]{2,1,0:T(8,128)(2,1)S(1)}, u32[]{:S(2)}, u32[]{:S(2)}) async-start(bf16[32,16,256]{2,1,0:T(8,128)(2,1)} %bitcast.14), calls=%async_computation.3 | async-start | bytes 524288 | tf_op jit(solution)/shard_map/all_to_all | solution.py:119
  114.2 1.2 fusion.59
  115.4 2.2 convolution_add_fusion.5
  117.6 7.7 %all-to-all-done.3 = bf16[32,16,256]{2,1,0:T(8,128)(2,1)S(1)} async-done(((bf16[32,16,256]{2,1,0:T(8,128)(2,1)}), bf16[32,16,256]{2,1,0:T(8,128)(2,1)S(1)}, u32[]{:S(2)}, u32[]{:S(2)}) %all-to-all-start.3) | async-done | bytes 262176 | tf_op jit(solution)/shard_map/all_to_all | solution.py:119
  126.9 1.2 fusion.64
  128.1 1.2 fusion.63
  129.3 1.2 convolution_add_fusion.2
  131.5 2.6 multiply_add_fusion
  134.0 0.8 fusion.105
  134.9 0.8 fusion.107
  135.8 1.1 convolution_add_fusion.3
  136.8 0.9 convolution_subtract_fusion.6
  137.7 0.9 fusion.38
  138.6 1.6 fusion.19
  140.2 2.0 copy.167
  142.2 1.4 copy.262
  143.7 14.7 %all_to_all.84 = bf16[16,32,256]{2,0,1:T(8,128)(2,1)S(1)} all-to-all(bf16[16,32,256]{2,0,1:T(8,128)(2,1)S(1)} %bitcast.214), channel_id=1, replica_groups=mesh['ctx'=32,'tp'=8] {'ctx'}, dimensions={1} | all-to-all | bytes 524288 | tf_op jit(solution)/shard_map/all_to_all | solution.py:124
  158.4 0.9 convert_element_type.263
  159.3 2.0 copy.169
  161.3 5.2 %fusion = bf16[4096,512]{0,1:T(8,128)(2,1)} fusion(bf16[4096,256]{1,0:T(8,128)(2,1)} %all-gather.2.cloned.1.call-done, f32[512,256]{0,1:T(8,128)} %copy.169, bf16[512,256]{0,1:T(8,128)(2,1)} %copy-done.8), kind=kOutput, calls=%fused_computation.1 | convolution fusion | flops 1076232192 | bytes 7077888 | tf_op jit(solution)/shard_map/dot_general | solution.py:149
  166.5 6.5 %copy.226 = bf16[4096,512]{1,0:T(8,128)(2,1)} copy(bf16[4096,512]{0,1:T(8,128)(2,1)} %fusion) | data formatting | bytes 8388608
  173.1 1.8 fusion.306
  175.5 0.8 fusion.97
  176.3 0.8 fusion.99
  177.2 0.9 convolution_add_fusion.1
  178.1 0.9 convolution_subtract_fusion.3
  178.9 0.8 fusion.31
  179.8 0.8 fusion.18
  182.0 4.1 %all-to-all-start.4 = ((bf16[16,32,256]{2,0,1:T(8,128)(2,1)}), bf16[16,32,256]{2,0,1:T(8,128)(2,1)S(1)}, u32[]{:S(2)}, u32[]{:S(2)}) async-start(bf16[16,32,256]{2,0,1:T(8,128)(2,1)} %bitcast.190), calls=%async_computation.4 | async-start | bytes 524288 | tf_op jit(solution)/shard_map/all_to_all | solution.py:125
  186.1 0.8 fusion.94
  187.0 0.8 fusion.92
  187.9 0.9 convolution_subtract_fusion.1
  188.7 0.9 convolution_add_fusion
  189.6 0.8 fusion.24
  190.4 0.8 fusion.17
  192.7 5.6 %all-to-all-done.4 = bf16[16,32,256]{2,0,1:T(8,128)(2,1)S(1)} async-done(((bf16[16,32,256]{2,0,1:T(8,128)(2,1)}), bf16[16,32,256]{2,0,1:T(8,128)(2,1)S(1)}, u32[]{:S(2)}, u32[]{:S(2)}) %all-to-all-start.4) | async-done | bytes 262176 | tf_op jit(solution)/shard_map/all_to_all | solution.py:125
  198.3 3.9 %all-to-all-start.5 = ((bf16[16,32,256]{2,0,1:T(8,128)(2,1)}), bf16[16,32,256]{2,0,1:T(8,128)(2,1)S(1)}, u32[]{:S(2)}, u32[]{:S(2)}) async-start(bf16[16,32,256]{2,0,1:T(8,128)(2,1)} %bitcast.189), calls=%async_computation.5 | async-start | bytes 524288 | tf_op jit(solution)/shard_map/all_to_all | solution.py:127
  203.5 1.3 collective-permute-start
  204.9 8.4 %all-to-all-done.5 = bf16[16,32,256]{2,0,1:T(8,128)(2,1)S(1)} async-done(((bf16[16,32,256]{2,0,1:T(8,128)(2,1)}), bf16[16,32,256]{2,0,1:T(8,128)(2,1)S(1)}, u32[]{:S(2)}, u32[]{:S(2)}) %all-to-all-start.5) | async-done | bytes 262176 | tf_op jit(solution)/shard_map/all_to_all | solution.py:127
  213.3 0.9 convert_element_type.265
  214.4 1.3 fusion.2
  215.7 1.2 copy.194
  216.8 104.7 %reduce-scatter.4.cloned.1.call-done = bf16[128,512]{1,0:T(8,128)(2,1)} async-done(((bf16[4096,512]{1,0:T(8,128)(2,1)}), bf16[128,512]{1,0:T(8,128)(2,1)}) %reduce-scatter.4.cloned.1.call-update) | async-done | bytes 131088
  321.5 1.0 copy.227
  322.6 0.8 copy.195
  (75 shorter events, 10.2 us)
Async XLA Ops:
  8.3 12.3 %copy-start.10 = (bf16[512,256]{1,0:T(8,128)(2,1)S(1)}, bf16[512,256]{1,0:T(8,128)(2,1)}, u32[]{:S(2)}) copy-start(bf16[512,256]{1,0:T(8,128)(2,1)} %param.8) | copy-start | bytes 786436
  9.4 20.8 %copy-start.6 = (bf16[512,256]{0,1:T(8,128)(2,1)}, bf16[512,256]{0,1:T(8,128)(2,1)S(1)}, u32[]{:S(2)}) copy-start(bf16[512,256]{0,1:T(8,128)(2,1)S(1)} %copy.152) | copy-start | bytes 786436
  10.3 19.9 %all-to-all-start.1 = ((bf16[32,16,256]{2,1,0:T(8,128)(2,1)}), bf16[32,16,256]{2,1,0:T(8,128)(2,1)S(1)}, u32[]{:S(2)}, u32[]{:S(2)}) async-start(bf16[32,16,256]{2,1,0:T(8,128)(2,1)} %bitcast.6), calls=%async_computation.1 | async-start | bytes 524288 | tf_op jit(solution)/shard_map/all_to_all | solution.py:118
  19.1 84.4 %all-gather.2.cloned.1.call-start = ((), (), s32[]{:S(2)}) async-start(), calls=%async_computation.7 | async-start | bytes 2359296 | tf_op jit(solution)/shard_map/all_gather | solution.py:108
  20.7 82.8 %copy-start.8 = (bf16[512,256]{0,1:T(8,128)(2,1)}, bf16[512,256]{0,1:T(8,128)(2,1)S(1)}, u32[]{:S(2)}) copy-start(bf16[512,256]{0,1:T(8,128)(2,1)S(1)} %copy.170) | copy-start | bytes 786436
  30.2 25.4 %all-to-all-start = ((f32[32,16,256]{2,1,0:T(8,128)}), f32[32,16,256]{2,1,0:T(8,128)S(1)}, u32[]{:S(2)}, u32[]{:S(2)}) async-start(f32[32,16,256]{2,1,0:T(8,128)} %bitcast), calls=%async_computation | async-start | bytes 1048576 | tf_op jit(solution)/shard_map/all_to_all | solution.py:121
  109.5 15.8 %all-to-all-start.3 = ((bf16[32,16,256]{2,1,0:T(8,128)(2,1)}), bf16[32,16,256]{2,1,0:T(8,128)(2,1)S(1)}, u32[]{:S(2)}, u32[]{:S(2)}) async-start(bf16[32,16,256]{2,1,0:T(8,128)(2,1)} %bitcast.14), calls=%async_computation.3 | async-start | bytes 524288 | tf_op jit(solution)/shard_map/all_to_all | solution.py:119
  114.2 207.4 %reduce-scatter.4.cloned.1.call-start = ((), (), s32[]{:S(2)}) async-start(), calls=%async_computation.8 | async-start | bytes 4325376
  129.3 1.2 copy-start.2
  129.3 1.5 copy-start.3
  129.3 1.8 copy-start.4
  129.3 2.1 copy-start.5
  173.0 3.3 copy-start
  182.0 16.3 %all-to-all-start.4 = ((bf16[16,32,256]{2,0,1:T(8,128)(2,1)}), bf16[16,32,256]{2,0,1:T(8,128)(2,1)S(1)}, u32[]{:S(2)}, u32[]{:S(2)}) async-start(bf16[16,32,256]{2,0,1:T(8,128)(2,1)} %bitcast.190), calls=%async_computation.4 | async-start | bytes 524288 | tf_op jit(solution)/shard_map/all_to_all | solution.py:125
  192.0 10.5 %copy-start.7 = (bf16[512,256]{0,1:T(8,128)(2,1)S(1)}, bf16[512,256]{0,1:T(8,128)(2,1)}, u32[]{:S(2)}) copy-start(bf16[512,256]{0,1:T(8,128)(2,1)} %copy-done.6) | copy-start | bytes 786436
  198.3 15.0 %all-to-all-start.5 = ((bf16[16,32,256]{2,0,1:T(8,128)(2,1)}), bf16[16,32,256]{2,0,1:T(8,128)(2,1)S(1)}, u32[]{:S(2)}, u32[]{:S(2)}) async-start(bf16[16,32,256]{2,0,1:T(8,128)(2,1)} %bitcast.189), calls=%async_computation.5 | async-start | bytes 524288 | tf_op jit(solution)/shard_map/all_to_all | solution.py:127
  202.2 1.0 copy-start.1
  202.2 1.2 copy-start.9
  202.5 2.3 copy-start.14
  202.5 2.3 copy-start.15
  202.5 2.3 copy-start.13
  203.5 10.6 %collective-permute-start = (bf16[3,512,6]{1,2,0:T(8,128)(2,1)S(1)}, bf16[3,512,6]{1,2,0:T(8,128)(2,1)S(1)}, u32[]{:S(2)}, u32[]{:S(2)}) collective-permute-start(bf16[3,512,6]{1,2,0:T(8,128)(2,1)S(1)} %pad_maximum_fusion), channel_id=1, source_target_pairs={{8,0},{16,8},{24,16},{32,24},{40,32},{48,40},{56,48},{64,56},{72,6... | collective-permute-start | bytes 55304 | tf_op jit(solution)/shard_map/ppermute | solution.py:14
  204.8 9.5 %copy-start.11 = (f32[3,512]{1,0:T(4,128)S(1)}, f32[3,512]{1,0:T(4,128)}, u32[]{:S(2)}) copy-start(f32[3,512]{1,0:T(4,128)} %get-tuple-element.40) | copy-start | bytes 18436
  204.8 9.5 %copy-start.12 = (f32[3,512]{1,0:T(4,128)S(1)}, f32[3,512]{1,0:T(4,128)}, u32[]{:S(2)}) copy-start(f32[3,512]{1,0:T(4,128)} %get-tuple-element.41) | copy-start | bytes 18436
Sparse Core Ops, SparseCore 0:
  22.6 80.8 all-gather.1
  173.2 148.3 reduce-scatter.3
where the time goes:
time: 334 us; the launch traced here: 331 us
  waiting for transfers between devices  191 us (57%)
  matrix products  51.5 us (15%)
  starting transfers between devices  27.2 us (8%)
  local copies, waits for them, and re-layouts  26.9 us (8%)
  between operations  15.2 us (5%)
  blocking collectives  14.7 us (4%)
  other arithmetic  4.05 us (1%)
    unnamed x3, waiting for transfers between devices  105 us
    all_gather x1, waiting for transfers between devices, local(): gathered = lax.all_gather(out_cotangent, 'tp', axis=0, tiled=True)  41.9 us
    unnamed x52, local copies, waits for them, and re-layouts  16.8 us
    all_to_all x1, blocking collectives, local(): lax.all_to_all(conv_cols, 'ctx', split_axis=1, concat_axis=0, tiled=True)  14.7 us
    all_to_all x1, waiting for transfers between devices, local(): lax.all_to_all(long_filter, 'ctx', split_axis=0, concat_axis=1, tiled=True)  12.6 us
    all_to_all x1, waiting for transfers between devices, local(): lax.all_to_all(kv_product, 'ctx', split_axis=0, concat_axis=1, tiled=True)  9.47 us
    all_to_all x1, starting transfers between devices, local(): lax.all_to_all(kv_product, 'ctx', split_axis=0, concat_axis=1, tiled=True)  8.75 us
    all_to_all x1, waiting for transfers between devices, local(): lax.all_to_all(corr_cols.astype(jnp.bfloat16), 'ctx', split_axis=1, conca...  8.42 us
  transfers between devices with their start and end apart: 8, of which 7 were waited for; matrix products, arithmetic and copies ran while one was open for 11% of the time, Pallas kernels for 0%

commit v1 on v0

v1 whole, which is shorter than its diff:
```python
import math

import jax
import jax.numpy as jnp
import ml_dtypes
import numpy as np
from jax import lax
from jax.experimental import pallas as pl
from jax.experimental.pallas import tpu as pltpu
from jax.sharding import PartitionSpec as P

BF = jnp.bfloat16
F32 = jnp.float32
NX, NZ, NY = 4, 4, 4
CTX, TP = 32, 8
CH = 16
LOC = 256
ROWS = 512
KP = 72
FINE = 128
TOTAL = 16384
VMEM = 44 * 1024 * 1024


def ctx_shift(dz, dx, dc):
    return [
        (z * 8 + x * 2 + c, (z + dz) % 4 * 8 + (x + dx) % 4 * 2 + (c + dc) % 2)
        for z in range(4)
        for x in range(4)
        for c in range(2)
    ]


def tp_shift(dy, dh):
    return [(y * 2 + h, (y + dy) % 4 * 2 + (h + dh) % 2) for y in range(4) for h in range(2)]


def split_np(table):
    high = table.astype(ml_dtypes.bfloat16)
    low = (table - high.astype(np.float64)).astype(ml_dtypes.bfloat16)
    return high, low


def make_tables():
    freq = np.arange(KP)[:, None]
    live = (freq <= 64).astype(np.float64)
    coarse = (2 * np.arange(32)[None, :] + np.arange(2)[:, None]).reshape(1, 64)
    angle = 2 * math.pi * ((freq * coarse) % 128) / 128
    first = np.concatenate([np.cos(angle) * live, -np.sin(angle) * live], 0)
    first = np.concatenate(split_np(first), 1)
    fine = np.arange(FINE)
    mid_angle = 2 * math.pi * ((fine[:, None] * fine[None, :]) % 128) / 128
    cos, sin = np.cos(mid_angle), np.sin(mid_angle)
    forward = np.stack(split_np(np.block([[cos, -sin], [sin, cos]])))
    inverse = np.stack(split_np(np.block([[cos, sin], [-sin, cos]])))
    tw_angle = 2 * math.pi * (freq * fine[None, :]) / TOTAL
    twiddle = np.stack([np.cos(tw_angle), np.sin(tw_angle)]).astype(np.float32)
    weight = np.where((freq == 0) | (freq == 64), 1.0, 2.0) * live / TOTAL
    last = np.concatenate([(np.cos(angle) * weight).T, (-np.sin(angle) * weight).T], 1)
    last = np.stack(split_np(last))
    return first, forward, inverse, twiddle, last


def halves(value):
    high = value.astype(BF)
    return high, (value - high.astype(F32)).astype(BF)


def mm(left, right):
    return jnp.dot(left, right, preferred_element_type=F32)


def mm_table(value, table_ref):
    high, low = halves(value)
    return mm(high, table_ref[0]) + mm(low, table_ref[0]) + mm(high, table_ref[1])


def forward_spectrum(block, first_ref, forward_ref, twiddle_ref, work_ref, spec_ref):
    chans = jnp.swapaxes(block.astype(F32), 0, 1).astype(BF)
    cos_tw, sin_tw = twiddle_ref[0], twiddle_ref[1]
    for pair in range(CH // 2):
        cols = []
        for chan in (2 * pair, 2 * pair + 1):
            both = jnp.concatenate([chans[chan, :, :FINE], chans[chan, :, FINE:]], 0)
            cols.append(jnp.concatenate([both, both], 0))
        coarse = mm(first_ref[...], jnp.concatenate(cols, 1))
        for which in range(2):
            real = coarse[:KP, which * FINE : (which + 1) * FINE]
            imag = coarse[KP:, which * FINE : (which + 1) * FINE]
            row = (2 * pair + which) * KP
            work_ref[row : row + KP, :FINE] = real * cos_tw + imag * sin_tw
            work_ref[row : row + KP, FINE:] = imag * cos_tw - real * sin_tw
    spec_ref[...] = mm_table(work_ref[...], forward_ref)


def inverse_signal(work_ref, inverse_ref, twiddle_ref, last_ref):
    work_ref[...] = mm_table(work_ref[...], inverse_ref)
    cos_tw, sin_tw = twiddle_ref[0], twiddle_ref[1]
    chans = []
    for pair in range(CH // 2):
        cols = []
        for chan in (2 * pair, 2 * pair + 1):
            real = work_ref[chan * KP : (chan + 1) * KP, :FINE]
            imag = work_ref[chan * KP : (chan + 1) * KP, FINE:]
            cols.append(
                jnp.concatenate(
                    [real * cos_tw - imag * sin_tw, imag * cos_tw + real * sin_tw], 0
                )
            )
        high, low = halves(jnp.concatenate(cols, 1))
        out = mm(last_ref[0], high) + mm(last_ref[0], low) + mm(last_ref[1], high)
        for which in range(2):
            mine = out[:, which * FINE : (which + 1) * FINE]
            chans.append(jnp.concatenate([mine[:32], mine[32:]], 1))
    return jnp.swapaxes(jnp.stack(chans, 0), 0, 1)


def times(left_ref, right_ref, sign_left, out_ref):
    lr, li = left_ref[:, :FINE], left_ref[:, FINE:]
    rr, ri = right_ref[:, :FINE], right_ref[:, FINE:]
    if sign_left > 0:
        out_ref[:, :FINE] = lr * rr - li * ri
        out_ref[:, FINE:] = lr * ri + li * rr
    else:
        out_ref[:, :FINE] = lr * rr + li * ri
        out_ref[:, FINE:] = lr * ri - li * rr


def prep_kernel(key_ref, value_ref, filter_ref, out_ref):
    kv = (key_ref[...].astype(F32) * value_ref[...].astype(F32)).astype(BF)
    out_ref[:, 0] = kv.reshape(CTX, CH, LOC)
    out_ref[:, 1] = filter_ref[...].astype(BF).reshape(CTX, CH, LOC)


def conv_kernel(in_ref, first, forward, inverse, twiddle, last, out_ref, kv_spec, fil_spec, work):
    forward_spectrum(in_ref[:, 0], first, forward, twiddle, work, kv_spec)
    forward_spectrum(in_ref[:, 1], first, forward, twiddle, work, fil_spec)
    times(fil_spec, kv_spec, 1, work)
    out_ref[...] = inverse_signal(work, inverse, twiddle, last).astype(BF)


def grad_kernel(
    in_ref, kv_spec, fil_spec, first, forward, inverse, twiddle, last, out_ref, spec, work
):
    forward_spectrum(in_ref[...], first, forward, twiddle, work, spec)
    times(fil_spec, spec, -1, work)
    out_ref[:, 0] = inverse_signal(work, inverse, twiddle, last).astype(BF)
    times(kv_spec, spec, -1, work)
    out_ref[:, 1] = inverse_signal(work, inverse, twiddle, last).astype(BF)


def inner_kernel(place_ref, weight_ref, query_ref, *refs):
    pieces = refs[:TP]
    inner_ref, gated_ref, keep_ref, send_ref = refs[TP:]
    core = place_ref[TP]
    total = jnp.zeros((ROWS, LOC), F32)
    for idx in range(TP):
        source = place_ref[idx]
        begin = pl.multiple_of(source * 512, 512)
        total = total + mm(weight_ref[:, pl.ds(begin, 512)], pieces[idx][...])
        for pair in range(2):
            slot = 2 * source + pair
            mine = pl.multiple_of(pair * 256 + core * 128, 128)
            other = pl.multiple_of(pair * 256 + (1 - core) * 128, 128)
            keep_ref[slot] = pieces[idx][pl.ds(mine, 128), :]
            send_ref[slot] = pieces[idx][pl.ds(other, 128), :]
    inner = total.astype(BF)
    inner_ref[...] = inner
    gated_ref[...] = (inner.astype(F32) * query_ref[...].astype(F32)).astype(BF)


def weight_kernel(place_ref, keep_ref, other_ref, mine_ref, sib_ref, own_ref, *outs):
    here = place_ref[0]
    for step in range(NX):
        want = lax.rem(here + step, NX)
        for z in range(NZ):
            slot = z * 4 + want
            part = lax.dot_general(
                keep_ref[slot], mine_ref[...], (((1,), (1,)), ((), ())), preferred_element_type=F32
            ) + lax.dot_general(
                other_ref[slot], sib_ref[...], (((1,), (1,)), ((), ())), preferred_element_type=F32
            )
            if step == 0:
                own_ref[z] = part
            else:
                outs[step - 1][z] = part.astype(BF)


def fold_kernel(place_ref, own_ref, one_ref, two_ref, three_ref, mine_ref, *outs):
    here = place_ref[1]
    for step in range(NZ):
        want = lax.rem(here + step, NZ)
        total = (
            own_ref[want]
            + one_ref[want].astype(F32)
            + two_ref[want].astype(F32)
            + three_ref[want].astype(F32)
        )
        if step == 0:
            mine_ref[...] = total
        else:
            outs[step - 1][...] = total.astype(BF)


def post_kernel(back_ref, inner_ref, conv_ref, key_ref, value_ref, post_ref, halo_ref, corr_ref):
    kv_grad = back_ref[:, 0].reshape(ROWS, LOC).astype(F32)
    grads = (
        inner_ref[...].astype(F32) * conv_ref[...].astype(F32),
        kv_grad * value_ref[...].astype(F32),
        kv_grad * key_ref[...].astype(F32),
    )
    lane = lax.broadcasted_iota(jnp.int32, (ROWS, FINE), 1)
    halo = jnp.zeros((ROWS, FINE), F32)
    for which in range(3):
        rounded = grads[which].astype(BF)
        post_ref[which] = rounded
        head = rounded[:, :FINE].astype(F32)
        if which:
            head = pltpu.roll(head, 8 * which, 1)
        halo = jnp.where((lane >= 8 * which) & (lane < 8 * which + 8), head, halo)
    halo_ref[...] = halo.astype(BF)
    corr_ref[...] = back_ref[:, 1].reshape(ROWS, LOC).astype(F32)


def feature_kernel(post_ref, halo_ref, taps_ref, out_ref):
    halo = halo_ref[...].astype(F32)
    for which in range(3):
        tail = halo if which == 0 else pltpu.roll(halo, FINE - 8 * which, 1)
        wide = jnp.concatenate([post_ref[which].astype(F32), tail], 1)
        taps = taps_ref[which]
        total = taps[:, 0:1] * wide[:, :LOC]
        for offset in range(1, 7):
            moved = pltpu.roll(wide, LOC + FINE - offset, 1)
            total = total + taps[:, offset : offset + 1] * moved[:, :LOC]
        out_ref[which] = total.astype(BF)


def call(kernel, outs, *args, scalars=0, scratch=(), name=None):
    specs = [pl.BlockSpec(memory_space=pltpu.SMEM)] * scalars
    specs += [pl.BlockSpec(memory_space=pltpu.VMEM)] * (len(args) - scalars)
    return pl.pallas_call(
        kernel,
        out_shape=[jax.ShapeDtypeStruct(shape, dtype) for shape, dtype in outs],
        in_specs=specs,
        out_specs=[pl.BlockSpec(memory_space=pltpu.VMEM)] * len(outs),
        scratch_shapes=list(scratch),
        compiler_params=pltpu.CompilerParams(vmem_limit_bytes=VMEM),
        name=name,
    )(*args)


def exchange(value):
    return lax.all_to_all(value, "ctx", split_axis=0, concat_axis=0, tiled=True)


def local(out_cotangent, query_rows, key_rows, value_rows, long_filter, short_filter, out_weight):
    ctx, tp = lax.axis_index("ctx"), lax.axis_index("tp")
    here_x, here_z, core = ctx // 2 % 4, ctx // 8, ctx % 2
    y, z_hi = tp // 2, tp % 2
    tables = [jnp.asarray(table) for table in make_tables()]

    far = lax.ppermute(out_cotangent, "tp", tp_shift(0, 1))
    pieces, sources = [out_cotangent, far], [tp, y * 2 + 1 - z_hi]
    for origin, flip in ((out_cotangent, 0), (far, 1)):
        for step in (1, 3, 2):
            pieces.append(lax.ppermute(origin, "tp", tp_shift(step, 0)))
            sources.append((y + 4 - step) % 4 * 2 + (z_hi + flip) % 2)
    place = jnp.stack(sources + [core]).astype(jnp.int32)

    (sent,) = call(
        prep_kernel, [((CTX, 2, CH, LOC), BF)], key_rows, value_rows, long_filter, name="prep"
    )
    weight_t = out_weight.T
    cols = exchange(sent)
    spec_shape = ((CH * KP, 2 * FINE), F32)
    conv_cols, kv_spec, fil_spec = call(
        conv_kernel,
        [((CTX, CH, LOC), BF), spec_shape, spec_shape],
        cols,
        *tables,
        scratch=[pltpu.VMEM(*spec_shape)],
        name="conv",
    )
    conv_out = exchange(conv_cols).reshape(ROWS, LOC)

    inner, gated, keep, send = call(
        inner_kernel,
        [((ROWS, LOC), BF), ((ROWS, LOC), BF), ((16, 128, LOC), BF), ((16, 128, LOC), BF)],
        place,
        weight_t,
        query_rows,
        *pieces,
        scalars=1,
        name="inner",
    )
    gated_cols = exchange(gated.reshape(CTX, CH, LOC))
    other = lax.ppermute(send, "ctx", ctx_shift(0, 0, 1))

    mixed = (query_rows.astype(F32) * conv_out.astype(F32)).astype(BF)
    mixed_sib = lax.ppermute(mixed, "ctx", ctx_shift(0, 0, 1))
    spot = jnp.stack([here_x, here_z]).astype(jnp.int32)
    part = (NZ, 128, 512)
    own, *to_x = call(
        weight_kernel,
        [(part, F32)] + [(part, BF)] * 3,
        spot,
        keep,
        other,
        mixed,
        mixed_sib,
        scalars=1,
        name="weight",
    )
    from_x = [
        lax.ppermute(to_x[step - 1], "ctx", ctx_shift(0, step, 0)) for step in (1, 2, 3)
    ]

    (back,) = call(
        grad_kernel,
        [((CTX, 2, CH, LOC), BF)],
        gated_cols,
        kv_spec,
        fil_spec,
        *tables,
        scratch=[pltpu.VMEM(*spec_shape), pltpu.VMEM(*spec_shape)],
        name="grad",
    )
    back = exchange(back)

    mine, *to_z = call(
        fold_kernel,
        [((128, 512), F32)] + [((128, 512), BF)] * 3,
        spot,
        own,
        *from_x,
        scalars=1,
        name="fold",
    )
    from_z = [
        lax.ppermute(to_z[step - 1], "ctx", ctx_shift(step, 0, 0)) for step in (1, 2, 3)
    ]
    out_weight_grad = mine + sum(value.astype(F32) for value in from_z)

    post, halo, filter_grad = call(
        post_kernel,
        [((3, ROWS, LOC), BF), ((ROWS, FINE), BF), ((ROWS, LOC), F32)],
        back,
        inner,
        conv_out,
        key_rows,
        value_rows,
        name="post",
    )
    halo = lax.ppermute(halo, "ctx", [(source, source - 1) for source in range(1, CTX)])
    (feature_grad,) = call(
        feature_kernel, [((3, ROWS, LOC), BF)], post, halo, short_filter, name="feature"
    )
    return (feature_grad, filter_grad, out_weight_grad)


def solution(mesh):
    return jax.shard_map(
        local,
        mesh=mesh,
        in_specs=(
            P("tp", "ctx"),
            P("tp", "ctx"),
            P("tp", "ctx"),
            P("tp", "ctx"),
            P("tp", "ctx"),
            P(None, "tp", None),
            P(None, "tp"),
        ),
        out_specs=(P(None, "tp", "ctx"), P("tp", "ctx"), P("ctx", "tp")),
        check_vma=False,
    )
```

time: 334 us -> 156 us (0.47)
  the two profiles are of different devices: /device:TPU:8 before, /device:TPU:39 now
where the time goes in v1:
time: 156 us; the launch traced here: 155 us
  starting transfers between devices  60.9 us (39%)
  waiting for transfers between devices  44.3 us (28%)
  Pallas kernels  25.1 us (16%)
  local copies, waits for them, and re-layouts  21.8 us (14%)
  other arithmetic  1.85 us (1%)
    all_to_all x4, starting transfers between devices, exchange(): return lax.all_to_all(value, 'ctx', split_axis=0, concat_axis=0, tiled=True)  39.4 us
    pallas_call x8, Pallas kernels, call(): pl.pallas_call(kernel, out_shape=[jax.ShapeDtypeStruct(shape, dtype) for...  25.1 us
    unnamed x42, local copies, waits for them, and re-layouts  21.7 us
    ppermute x3, waiting for transfers between devices, local(): lax.ppermute(to_x[step - 1], 'ctx', ctx_shift(0, step, 0))  17.6 us
    ppermute x6, starting transfers between devices, local(): pieces.append(lax.ppermute(origin, 'tp', tp_shift(step, 0)))  8.76 us
    ppermute x1, waiting for transfers between devices, local(): far = lax.ppermute(out_cotangent, 'tp', tp_shift(0, 1))  8.23 us
    all_to_all x4, waiting for transfers between devices, exchange(): return lax.all_to_all(value, 'ctx', split_axis=0, concat_axis=0, tiled=True)  7.75 us
    ppermute x3, waiting for transfers between devices, local(): lax.ppermute(to_z[step - 1], 'ctx', ctx_shift(step, 0, 0))  5.75 us
  transfers between devices with their start and end apart: 20, of which 11 were waited for; matrix products, arithmetic and copies ran while one was open for 6% of the time, Pallas kernels for 16%

profile of v1, /device:TPU:39, one launch (start us, length us, event | category | flops | bytes accessed | tf_op | source)
XLA Modules:
  0.0 154.8 jit_solution(7507813345453169596)
XLA Ops:
  0.6 0.0 copy-start.5
  0.6 0.9 copy-done.5
  1.6 0.9 copy-done.7
  2.5 1.0 copy-done.10
  3.6 0.9 prep.1
  4.5 8.9 %all-to-all-start.1 = ((bf16[32,2,16,256]{3,2,1,0:T(8,128)(2,1)}), bf16[32,2,16,256]{3,2,1,0:T(8,128)(2,1)S(1)}, u32[]{:S(2)}, u32[]{:S(2)}) async-start(bf16[32,2,16,256]{3,2,1,0:T(8,128)(2,1)} %prep.1), calls=%async_computation.1 | async-start | bytes 1048576 | tf_op jit(solution)/shard_map/all_to_all | solution.py:253
  13.3 4.3 %collective-permute-start = (bf16[512,256]{1,0:T(8,128)(2,1)}, bf16[512,256]{1,0:T(8,128)(2,1)S(1)}, u32[]{:S(2)}, u32[]{:S(2)}) collective-permute-start(bf16[512,256]{1,0:T(8,128)(2,1)} %refs_0_.1), channel_id=1, source_target_pairs={{0,1},{1,0},{2,3},{3,2},{4,5},{5,4},{6,7},{7,6},{8,9},{9,8},{10,11... | collective-permute-start | bytes 786440 | tf_op jit(solution)/shard_map/ppermute | solution.py:262
  17.6 1.3 collective-permute-start.1
  18.9 1.4 collective-permute-start.2
  20.4 1.6 %collective-permute-start.3 = (bf16[512,256]{1,0:T(8,128)(2,1)}, bf16[512,256]{1,0:T(8,128)(2,1)S(1)}, u32[]{:S(2)}, u32[]{:S(2)}) collective-permute-start(bf16[512,256]{1,0:T(8,128)(2,1)} %refs_0_.1), channel_id=1, source_target_pairs={{0,4},{1,5},{2,6},{3,7},{4,0},{5,1},{6,2},{7,3},{8,12},{9,13},{10,... | collective-permute-start | bytes 786440 | tf_op jit(solution)/shard_map/ppermute | solution.py:266
  22.0 8.2 %collective-permute-done.refs_1_ = bf16[512,256]{1,0:T(8,128)(2,1)S(1)} collective-permute-done((bf16[512,256]{1,0:T(8,128)(2,1)}, bf16[512,256]{1,0:T(8,128)(2,1)S(1)}, u32[]{:S(2)}, u32[]{:S(2)}) %collective-permute-start) | collective-permute-done | bytes 262176 | tf_op jit(solution)/shard_map/ppermute | solution.py:262
  30.2 1.3 collective-permute-start.4
  31.5 1.4 collective-permute-start.5
  33.0 1.6 %collective-permute-start.6 = (bf16[512,256]{1,0:T(8,128)(2,1)S(1)}, bf16[512,256]{1,0:T(8,128)(2,1)S(1)}, u32[]{:S(2)}, u32[]{:S(2)}) collective-permute-start(bf16[512,256]{1,0:T(8,128)(2,1)S(1)} %collective-permute-done.refs_1_), channel_id=1, source_target_pairs={{0,4},{1,5},{2,6},{3,7},{4,0},{5,1},{6,2},{7,3},{8,12},{9,13},{10,... | collective-permute-start | bytes 786440 | tf_op jit(solution)/shard_map/ppermute | solution.py:266
  34.6 0.0 copy-start.11
  34.6 0.0 copy-start.12
  34.7 6.5 %copy.15 = bf16[4096,512]{0,1:T(8,128)(2,1)} copy(bf16[4096,512]{1,0:T(8,128)(2,1)} %param.18) | data formatting | bytes 8388608 | tf_op args[6]
  41.2 0.1 stack.48.place_ref
  41.3 3.9 %collective-permute-done.6.refs_7_ = bf16[512,256]{1,0:T(8,128)(2,1)S(1)} collective-permute-done((bf16[512,256]{1,0:T(8,128)(2,1)S(1)}, bf16[512,256]{1,0:T(8,128)(2,1)S(1)}, u32[]{:S(2)}, u32[]{:S(2)}) %collective-permute-start.6) | collective-permute-done | bytes 262176 | tf_op jit(solution)/shard_map/ppermute | solution.py:266
  45.2 2.2 %copy-done = bf16[4096,512]{0,1:T(8,128)(2,1)S(1)} copy-done((bf16[4096,512]{0,1:T(8,128)(2,1)S(1)}, bf16[4096,512]{0,1:T(8,128)(2,1)}, u32[]{:S(2)}) %copy-start) | copy-done | bytes 4194328
  47.4 2.6 %inner.1 = (bf16[512,256]{1,0:T(8,128)(2,1)S(1)}, bf16[512,256]{1,0:T(8,128)(2,1)}, bf16[16,128,256]{2,1,0:T(8,128)(2,1)S(1)}, bf16[16,128,256]{2,1,0:T(8,128)(2,1)S(1)}) custom-call(s32[9]{0:T(128)S(1)} %stack.48.place_ref, bf16[512,4096]{1,0:T(8,128)(2,1)S(1)} %bitcast.15, bf16[512,256]{1,0:T(8,128)(2,1)S(1)} %copy-done.9, ...), custom_call_target="tpu_custom_call" | custom-call | tf_op jit(solution)/shard_map/inner/pallas_call | solution.py:241
  50.0 1.0 copy-done.3
  51.0 0.7 copy-done.14
  51.7 1.0 copy-done.19
  52.7 17.1 %all-to-all-start = ((bf16[32,16,256]{2,1,0:T(8,128)(2,1)}), bf16[32,16,256]{2,1,0:T(8,128)(2,1)}, u32[]{:S(2)}, u32[]{:S(2)}) async-start(bf16[32,16,256]{2,1,0:T(8,128)(2,1)} %bitcast.10), calls=%async_computation | async-start | bytes 524288 | tf_op jit(solution)/shard_map/all_to_all | solution.py:253
  69.7 0.4 collective-permute-start.8
  70.2 0.0 copy-start.17
  70.2 0.8 copy-done.17
  71.0 3.0 %conv.1 = (bf16[32,16,256]{2,1,0:T(8,128)(2,1)S(1)}, f32[1152,256]{1,0:T(8,128)S(1)}, f32[1152,256]{1,0:T(8,128)S(1)}) custom-call(bf16[32,2,16,256]{3,2,1,0:T(8,128)(2,1)S(1)} %all-to-all-done.1.in_ref, bf16[144,128]{1,0:T(8,128)(2,1)S(1)} %copy-done.17, bf16[2,256,256]{2,1,0:T(8,128)(2,1)S(1)} %copy-done.1, bf16[2,256,256]{2,1,0:T(8,128)(2,1)S(1)} %copy-done.2, ...), custom_call_target="tpu_custom_call" | custom-call | tf_op jit(solution)/shard_map/conv/pallas_call | solution.py:241
  74.0 0.0 copy-start.13
  74.0 0.7 copy-done.13
  74.7 3.3 %all-to-all-done.in_ref = bf16[32,16,256]{2,1,0:T(8,128)(2,1)} async-done(((bf16[32,16,256]{2,1,0:T(8,128)(2,1)}), bf16[32,16,256]{2,1,0:T(8,128)(2,1)}, u32[]{:S(2)}, u32[]{:S(2)}) %all-to-all-start) | async-done | bytes 262176 | tf_op jit(solution)/shard_map/all_to_all | solution.py:253
  78.0 6.7 %all-to-all-start.3 = ((bf16[32,16,256]{2,1,0:T(8,128)(2,1)}), bf16[32,16,256]{2,1,0:T(8,128)(2,1)S(1)}, u32[]{:S(2)}, u32[]{:S(2)}) async-start(bf16[32,16,256]{2,1,0:T(8,128)(2,1)} %copy-done.13), calls=%async_computation.3 | async-start | bytes 524288 | tf_op jit(solution)/shard_map/all_to_all | solution.py:253
  84.8 0.0 copy-start.18
  84.8 0.8 copy-done.18
  85.5 5.1 %grad.1 = bf16[32,2,16,256]{3,2,1,0:T(8,128)(2,1)} custom-call(bf16[32,16,256]{2,1,0:T(8,128)(2,1)} %all-to-all-done.in_ref, f32[1152,256]{1,0:T(8,128)S(1)} %get-tuple-element.22.kv_spec, f32[1152,256]{1,0:T(8,128)S(1)} %get-tuple-element.23.fil_spec, bf16[144,128]{1,0:T(8,128)(2,1)S(1)} %copy-done.18, bf16[2,256,256]{2,1,0:T(8,128)(2,1)S(1)} %copy-done.1, ...), custom_call_target="tpu_custom_call" | custom-call | tf_op jit(solution)/shard_map/grad/pallas_call | solution.py:241
  90.7 2.3 %all-to-all-done.3 = bf16[32,16,256]{2,1,0:T(8,128)(2,1)S(1)} async-done(((bf16[32,16,256]{2,1,0:T(8,128)(2,1)}), bf16[32,16,256]{2,1,0:T(8,128)(2,1)S(1)}, u32[]{:S(2)}, u32[]{:S(2)}) %all-to-all-start.3) | async-done | bytes 262176 | tf_op jit(solution)/shard_map/all_to_all | solution.py:253
  93.0 6.8 %all-to-all-start.2 = ((bf16[32,2,16,256]{3,2,1,0:T(8,128)(2,1)}), bf16[32,2,16,256]{3,2,1,0:T(8,128)(2,1)S(1)}, u32[]{:S(2)}, u32[]{:S(2)}) async-start(bf16[32,2,16,256]{3,2,1,0:T(8,128)(2,1)} %grad.1), calls=%async_computation.2 | async-start | bytes 1048576 | tf_op jit(solution)/shard_map/all_to_all | solution.py:253
  99.7 1.0 multiply_convert_fusion.mine_ref
  100.8 0.4 collective-permute-start.9
  101.2 0.1 pad_add_fusion.place_ref
  101.3 1.1 collective-permute-done.9.sib_ref
  102.4 1.2 copy-done.4
  103.6 4.9 %weight.1 = (f32[4,128,512]{2,1,0:T(8,128)S(1)}, bf16[4,128,512]{2,1,0:T(8,128)(2,1)}, bf16[4,128,512]{2,1,0:T(8,128)(2,1)}, bf16[4,128,512]{2,1,0:T(8,128)(2,1)}) custom-call(s32[2]{0:T(128)S(1)} %pad_add_fusion.place_ref, bf16[16,128,256]{2,1,0:T(8,128)(2,1)S(1)} %copy-done.4, bf16[16,128,256]{2,1,0:T(8,128)(2,1)} %collective-permute-done.8.other_ref, ...), custom_call_target="tpu_custom_call" | custom-call | tf_op jit(solution)/shard_map/weight/pallas_call | solution.py:241
  108.5 0.2 collective-permute-start.10
  108.7 2.1 %collective-permute-start.11 = (bf16[4,128,512]{2,1,0:T(8,128)(2,1)}, bf16[4,128,512]{2,1,0:T(8,128)(2,1)}, u32[]{:S(2)}, u32[]{:S(2)}) collective-permute-start(bf16[4,128,512]{2,1,0:T(8,128)(2,1)} %get-tuple-element.33), channel_id=1, source_target_pairs={{0,32},{8,40},{16,48},{24,56},{32,0},{40,8},{48,16},{56,24},{64,96... | collective-permute-start | bytes 1572872 | tf_op jit(solution)/shard_map/ppermute | solution.py:315
  110.8 2.1 %all-to-all-done.2.back_ref = bf16[32,2,16,256]{3,2,1,0:T(8,128)(2,1)S(1)} async-done(((bf16[32,2,16,256]{3,2,1,0:T(8,128)(2,1)}), bf16[32,2,16,256]{3,2,1,0:T(8,128)(2,1)S(1)}, u32[]{:S(2)}, u32[]{:S(2)}) %all-to-all-start.2) | async-done | bytes 524320 | tf_op jit(solution)/shard_map/all_to_all | solution.py:253
  112.9 0.9 copy-done.6
  113.9 0.9 copy-done.8
  114.8 0.9 copy-done.15
  115.8 1.1 post.1
  116.9 2.9 %collective-permute-start.7 = (bf16[512,128]{1,0:T(8,128)(2,1)}, bf16[512,128]{1,0:T(8,128)(2,1)S(1)}, u32[]{:S(2)}, u32[]{:S(2)}) collective-permute-start(bf16[512,128]{1,0:T(8,128)(2,1)} %get-tuple-element.27), channel_id=1, source_target_pairs={{8,0},{16,8},{24,16},{32,24},{40,32},{48,40},{56,48},{64,56},{72,6... | collective-permute-start | bytes 393224 | tf_op jit(solution)/shard_map/ppermute | solution.py:354
  119.8 2.8 %collective-permute-done.10.one_ref = bf16[4,128,512]{2,1,0:T(8,128)(2,1)S(1)} collective-permute-done((bf16[4,128,512]{2,1,0:T(8,128)(2,1)}, bf16[4,128,512]{2,1,0:T(8,128)(2,1)S(1)}, u32[]{:S(2)}, u32[]{:S(2)}) %collective-permute-start.10) | collective-permute-done | bytes 524320 | tf_op jit(solution)/shard_map/ppermute | solution.py:315
  122.6 1.5 collective-permute-done.11.two_ref
  124.1 13.3 %collective-permute-done.12.three_ref = bf16[4,128,512]{2,1,0:T(8,128)(2,1)} collective-permute-done((bf16[4,128,512]{2,1,0:T(8,128)(2,1)}, bf16[4,128,512]{2,1,0:T(8,128)(2,1)}, u32[]{:S(2)}, u32[]{:S(2)}) %collective-permute-start.12) | collective-permute-done | bytes 524320 | tf_op jit(solution)/shard_map/ppermute | solution.py:315
  137.4 2.0 %fold.1 = (f32[128,512]{1,0:T(8,128)S(1)}, bf16[128,512]{1,0:T(8,128)(2,1)S(1)}, bf16[128,512]{1,0:T(8,128)(2,1)S(1)}, bf16[128,512]{1,0:T(8,128)(2,1)}) custom-call(s32[2]{0:T(128)S(1)} %pad_add_fusion.place_ref, f32[4,128,512]{2,1,0:T(8,128)S(1)} %get-tuple-element.31.own_ref, bf16[4,128,512]{2,1,0:T(8,128)(2,1)S(1)} %collective-permute-done.10.one_ref, ...), custom_call_target="tpu_custom_call" | custom-call | tf_op jit(solution)/shard_map/fold/pallas_call | solution.py:241
  139.4 0.9 collective-permute-start.13
  140.3 1.4 collective-permute-start.14
  141.7 0.0 collective-permute-start.15
  141.7 1.1 copy.16.taps_ref
  142.8 5.5 %feature.1 = bf16[3,512,256]{2,1,0:T(8,128)(2,1)} custom-call(bf16[3,512,256]{2,1,0:T(8,128)(2,1)S(1)} %get-tuple-element.26.post_ref, bf16[512,128]{1,0:T(8,128)(2,1)S(1)} %collective-permute-done.7.halo_ref, f32[3,512,7]{2,1,0:T(8,128)S(1)} %copy.16.taps_ref), custom_call_target="tpu_custom_call" | custom-call | tf_op jit(solution)/shard_map/feature/pallas_call | solution.py:241
  148.3 2.8 %collective-permute-done.14 = bf16[128,512]{1,0:T(8,128)(2,1)S(1)} collective-permute-done((bf16[128,512]{1,0:T(8,128)(2,1)S(1)}, bf16[128,512]{1,0:T(8,128)(2,1)S(1)}, u32[]{:S(2)}, u32[]{:S(2)}) %collective-permute-start.14) | collective-permute-done | bytes 131104 | tf_op jit(solution)/shard_map/ppermute | solution.py:340
  151.1 2.9 %collective-permute-done.15 = bf16[128,512]{1,0:T(8,128)(2,1)S(1)} collective-permute-done((bf16[128,512]{1,0:T(8,128)(2,1)}, bf16[128,512]{1,0:T(8,128)(2,1)S(1)}, u32[]{:S(2)}, u32[]{:S(2)}) %collective-permute-start.15) | collective-permute-done | bytes 131104 | tf_op jit(solution)/shard_map/ppermute | solution.py:340
  154.0 0.8 add_add_fusion
  (30 shorter events, 0.1 us)
Async XLA Ops:
  0.6 1.0 copy-start.5
  1.6 0.9 copy-start.7
  2.5 1.0 copy-start.10
  4.5 48.2 %all-to-all-start.1 = ((bf16[32,2,16,256]{3,2,1,0:T(8,128)(2,1)}), bf16[32,2,16,256]{3,2,1,0:T(8,128)(2,1)S(1)}, u32[]{:S(2)}, u32[]{:S(2)}) async-start(bf16[32,2,16,256]{3,2,1,0:T(8,128)(2,1)} %prep.1), calls=%async_computation.1 | async-start | bytes 1048576 | tf_op jit(solution)/shard_map/all_to_all | solution.py:253
  13.3 16.9 %collective-permute-start = (bf16[512,256]{1,0:T(8,128)(2,1)}, bf16[512,256]{1,0:T(8,128)(2,1)S(1)}, u32[]{:S(2)}, u32[]{:S(2)}) collective-permute-start(bf16[512,256]{1,0:T(8,128)(2,1)} %refs_0_.1), channel_id=1, source_target_pairs={{0,1},{1,0},{2,3},{3,2},{4,5},{5,4},{6,7},{7,6},{8,9},{9,8},{10,11... | collective-permute-start | bytes 786440 | tf_op jit(solution)/shard_map/ppermute | solution.py:262
  17.6 15.4 %collective-permute-start.1 = (bf16[512,256]{1,0:T(8,128)(2,1)}, bf16[512,256]{1,0:T(8,128)(2,1)S(1)}, u32[]{:S(2)}, u32[]{:S(2)}) collective-permute-start(bf16[512,256]{1,0:T(8,128)(2,1)} %refs_0_.1), channel_id=1, source_target_pairs={{0,2},{1,3},{2,4},{3,5},{4,6},{5,7},{6,0},{7,1},{8,10},{9,11},{10,... | collective-permute-start | bytes 786440 | tf_op jit(solution)/shard_map/ppermute | solution.py:266
  18.9 22.3 %collective-permute-start.2 = (bf16[512,256]{1,0:T(8,128)(2,1)}, bf16[512,256]{1,0:T(8,128)(2,1)S(1)}, u32[]{:S(2)}, u32[]{:S(2)}) collective-permute-start(bf16[512,256]{1,0:T(8,128)(2,1)} %refs_0_.1), channel_id=1, source_target_pairs={{0,6},{1,7},{2,0},{3,1},{4,2},{5,3},{6,4},{7,5},{8,14},{9,15},{10,... | collective-permute-start | bytes 786440 | tf_op jit(solution)/shard_map/ppermute | solution.py:266
  20.4 20.9 %collective-permute-start.3 = (bf16[512,256]{1,0:T(8,128)(2,1)}, bf16[512,256]{1,0:T(8,128)(2,1)S(1)}, u32[]{:S(2)}, u32[]{:S(2)}) collective-permute-start(bf16[512,256]{1,0:T(8,128)(2,1)} %refs_0_.1), channel_id=1, source_target_pairs={{0,4},{1,5},{2,6},{3,7},{4,0},{5,1},{6,2},{7,3},{8,12},{9,13},{10,... | collective-permute-start | bytes 786440 | tf_op jit(solution)/shard_map/ppermute | solution.py:266
  30.2 11.0 %collective-permute-start.4 = (bf16[512,256]{1,0:T(8,128)(2,1)S(1)}, bf16[512,256]{1,0:T(8,128)(2,1)S(1)}, u32[]{:S(2)}, u32[]{:S(2)}) collective-permute-start(bf16[512,256]{1,0:T(8,128)(2,1)S(1)} %collective-permute-done.refs_1_), channel_id=1, source_target_pairs={{0,2},{1,3},{2,4},{3,5},{4,6},{5,7},{6,0},{7,1},{8,10},{9,11},{10,... | collective-permute-start | bytes 786440 | tf_op jit(solution)/shard_map/ppermute | solution.py:266
  31.5 9.7 %collective-permute-start.5 = (bf16[512,256]{1,0:T(8,128)(2,1)S(1)}, bf16[512,256]{1,0:T(8,128)(2,1)S(1)}, u32[]{:S(2)}, u32[]{:S(2)}) collective-permute-start(bf16[512,256]{1,0:T(8,128)(2,1)S(1)} %collective-permute-done.refs_1_), channel_id=1, source_target_pairs={{0,6},{1,7},{2,0},{3,1},{4,2},{5,3},{6,4},{7,5},{8,14},{9,15},{10,... | collective-permute-start | bytes 786440 | tf_op jit(solution)/shard_map/ppermute | solution.py:266
  33.0 12.2 %collective-permute-start.6 = (bf16[512,256]{1,0:T(8,128)(2,1)S(1)}, bf16[512,256]{1,0:T(8,128)(2,1)S(1)}, u32[]{:S(2)}, u32[]{:S(2)}) collective-permute-start(bf16[512,256]{1,0:T(8,128)(2,1)S(1)} %collective-permute-done.refs_1_), channel_id=1, source_target_pairs={{0,4},{1,5},{2,6},{3,7},{4,0},{5,1},{6,2},{7,3},{8,12},{9,13},{10,... | collective-permute-start | bytes 786440 | tf_op jit(solution)/shard_map/ppermute | solution.py:266
  34.6 10.6 %copy-start.9 = (bf16[512,256]{1,0:T(8,128)(2,1)S(1)}, bf16[512,256]{1,0:T(8,128)(2,1)}, u32[]{:S(2)}) copy-start(bf16[512,256]{1,0:T(8,128)(2,1)} %query_ref.1) | copy-start | bytes 786436
  34.6 10.6 %copy-start.16 = (bf16[512,256]{1,0:T(8,128)(2,1)S(1)}, bf16[512,256]{1,0:T(8,128)(2,1)}, u32[]{:S(2)}) copy-start(bf16[512,256]{1,0:T(8,128)(2,1)} %refs_0_.1) | copy-start | bytes 786436
  34.6 35.6 %copy-start.1 = (bf16[2,256,256]{2,1,0:T(8,128)(2,1)S(1)}, bf16[2,256,256]{2,1,0:T(8,128)(2,1)}, u32[]{:S(2)}) copy-start(bf16[2,256,256]{2,1,0:T(8,128)(2,1)} %constant.117.clone.forward) | copy-start | bytes 786436
  34.6 35.6 %copy-start.2 = (bf16[2,256,256]{2,1,0:T(8,128)(2,1)S(1)}, bf16[2,256,256]{2,1,0:T(8,128)(2,1)}, u32[]{:S(2)}) copy-start(bf16[2,256,256]{2,1,0:T(8,128)(2,1)} %constant.118.clone.inverse) | copy-start | bytes 786436
  34.6 35.6 %copy-start.11 = (f32[2,72,128]{2,1,0:T(8,128)S(1)}, f32[2,72,128]{2,1,0:T(8,128)}, u32[]{:S(2)}) copy-start(f32[2,72,128]{2,1,0:T(8,128)} %constant.119.clone.twiddle) | copy-start | bytes 221188
  34.6 35.6 %copy-start.12 = (bf16[2,64,144]{2,1,0:T(8,128)(2,1)S(1)}, bf16[2,64,144]{2,1,0:T(8,128)(2,1)}, u32[]{:S(2)}) copy-start(bf16[2,64,144]{2,1,0:T(8,128)(2,1)} %constant.120.clone.last) | copy-start | bytes 110596
  45.2 2.2 %copy-start = (bf16[4096,512]{0,1:T(8,128)(2,1)S(1)}, bf16[4096,512]{0,1:T(8,128)(2,1)}, u32[]{:S(2)}) copy-start(bf16[4096,512]{0,1:T(8,128)(2,1)} %copy.15) | copy-start | bytes 12582916
  50.0 1.0 copy-start.3
  51.0 0.7 copy-start.14
  51.7 1.0 copy-start.19
  52.7 25.3 %all-to-all-start = ((bf16[32,16,256]{2,1,0:T(8,128)(2,1)}), bf16[32,16,256]{2,1,0:T(8,128)(2,1)}, u32[]{:S(2)}, u32[]{:S(2)}) async-start(bf16[32,16,256]{2,1,0:T(8,128)(2,1)} %bitcast.10), calls=%async_computation | async-start | bytes 524288 | tf_op jit(solution)/shard_map/all_to_all | solution.py:253
  69.7 31.5 %collective-permute-start.8 = (bf16[16,128,256]{2,1,0:T(8,128)(2,1)}, bf16[16,128,256]{2,1,0:T(8,128)(2,1)}, u32[]{:S(2)}, u32[]{:S(2)}) collective-permute-start(bf16[16,128,256]{2,1,0:T(8,128)(2,1)} %copy-done.19), channel_id=1, source_target_pairs={{0,8},{8,0},{16,24},{24,16},{32,40},{40,32},{48,56},{56,48},{64,72... | collective-permute-start | bytes 3145736 | tf_op jit(solution)/shard_map/ppermute | solution.py:297
  70.2 0.8 copy-start.17
  74.0 0.7 copy-start.13
  78.0 15.0 %all-to-all-start.3 = ((bf16[32,16,256]{2,1,0:T(8,128)(2,1)}), bf16[32,16,256]{2,1,0:T(8,128)(2,1)S(1)}, u32[]{:S(2)}, u32[]{:S(2)}) async-start(bf16[32,16,256]{2,1,0:T(8,128)(2,1)} %copy-done.13), calls=%async_computation.3 | async-start | bytes 524288 | tf_op jit(solution)/shard_map/all_to_all | solution.py:253
  84.8 0.8 copy-start.18
  93.0 20.0 %all-to-all-start.2 = ((bf16[32,2,16,256]{3,2,1,0:T(8,128)(2,1)}), bf16[32,2,16,256]{3,2,1,0:T(8,128)(2,1)S(1)}, u32[]{:S(2)}, u32[]{:S(2)}) async-start(bf16[32,2,16,256]{3,2,1,0:T(8,128)(2,1)} %grad.1), calls=%async_computation.2 | async-start | bytes 1048576 | tf_op jit(solution)/shard_map/all_to_all | solution.py:253
  100.8 1.6 %collective-permute-start.9 = (bf16[512,256]{1,0:T(8,128)(2,1)S(1)}, bf16[512,256]{1,0:T(8,128)(2,1)S(1)}, u32[]{:S(2)}, u32[]{:S(2)}) collective-permute-start(bf16[512,256]{1,0:T(8,128)(2,1)S(1)} %multiply_convert_fusion.mine_ref), channel_id=1, source_target_pairs={{0,8},{8,0},{16,24},{24,16},{32,40},{40,32},{48,56},{56,48},{64,72... | collective-permute-start | bytes 786440 | tf_op jit(solution)/shard_map/ppermute | solution.py:300
  102.4 1.2 copy-start.4
  108.5 14.1 %collective-permute-start.10 = (bf16[4,128,512]{2,1,0:T(8,128)(2,1)}, bf16[4,128,512]{2,1,0:T(8,128)(2,1)S(1)}, u32[]{:S(2)}, u32[]{:S(2)}) collective-permute-start(bf16[4,128,512]{2,1,0:T(8,128)(2,1)} %get-tuple-element.32), channel_id=1, source_target_pairs={{0,16},{8,24},{16,32},{24,40},{32,48},{40,56},{48,0},{56,8},{64,80... | collective-permute-start | bytes 1572872 | tf_op jit(solution)/shard_map/ppermute | solution.py:315
  108.7 15.4 %collective-permute-start.11 = (bf16[4,128,512]{2,1,0:T(8,128)(2,1)}, bf16[4,128,512]{2,1,0:T(8,128)(2,1)}, u32[]{:S(2)}, u32[]{:S(2)}) collective-permute-start(bf16[4,128,512]{2,1,0:T(8,128)(2,1)} %get-tuple-element.33), channel_id=1, source_target_pairs={{0,32},{8,40},{16,48},{24,56},{32,0},{40,8},{48,16},{56,24},{64,96... | collective-permute-start | bytes 1572872 | tf_op jit(solution)/shard_map/ppermute | solution.py:315
  110.8 26.5 %collective-permute-start.12 = (bf16[4,128,512]{2,1,0:T(8,128)(2,1)}, bf16[4,128,512]{2,1,0:T(8,128)(2,1)}, u32[]{:S(2)}, u32[]{:S(2)}) collective-permute-start(bf16[4,128,512]{2,1,0:T(8,128)(2,1)} %get-tuple-element.34), channel_id=1, source_target_pairs={{0,48},{8,56},{16,0},{24,8},{32,16},{40,24},{48,32},{56,40},{64,11... | collective-permute-start | bytes 1572872 | tf_op jit(solution)/shard_map/ppermute | solution.py:315
  112.9 1.0 copy-start.6
  113.9 0.9 copy-start.8
  114.8 0.9 copy-start.15
  116.9 25.9 %collective-permute-start.7 = (bf16[512,128]{1,0:T(8,128)(2,1)}, bf16[512,128]{1,0:T(8,128)(2,1)S(1)}, u32[]{:S(2)}, u32[]{:S(2)}) collective-permute-start(bf16[512,128]{1,0:T(8,128)(2,1)} %get-tuple-element.27), channel_id=1, source_target_pairs={{8,0},{16,8},{24,16},{32,24},{40,32},{48,40},{56,48},{64,56},{72,6... | collective-permute-start | bytes 393224 | tf_op jit(solution)/shard_map/ppermute | solution.py:354
  139.4 8.9 %collective-permute-start.13 = (bf16[128,512]{1,0:T(8,128)(2,1)S(1)}, bf16[128,512]{1,0:T(8,128)(2,1)S(1)}, u32[]{:S(2)}, u32[]{:S(2)}) collective-permute-start(bf16[128,512]{1,0:T(8,128)(2,1)S(1)} %get-tuple-element.36), channel_id=1, source_target_pairs={{0,64},{8,72},{16,80},{24,88},{32,96},{40,104},{48,112},{56,120},{... | collective-permute-start | bytes 393224 | tf_op jit(solution)/shard_map/ppermute | solution.py:340
  140.3 10.8 %collective-permute-start.14 = (bf16[128,512]{1,0:T(8,128)(2,1)S(1)}, bf16[128,512]{1,0:T(8,128)(2,1)S(1)}, u32[]{:S(2)}, u32[]{:S(2)}) collective-permute-start(bf16[128,512]{1,0:T(8,128)(2,1)S(1)} %get-tuple-element.37), channel_id=1, source_target_pairs={{0,128},{8,136},{16,144},{24,152},{32,160},{40,168},{48,176},{56,1... | collective-permute-start | bytes 393224 | tf_op jit(solution)/shard_map/ppermute | solution.py:340
  141.7 12.4 %collective-permute-start.15 = (bf16[128,512]{1,0:T(8,128)(2,1)}, bf16[128,512]{1,0:T(8,128)(2,1)S(1)}, u32[]{:S(2)}, u32[]{:S(2)}) collective-permute-start(bf16[128,512]{1,0:T(8,128)(2,1)} %get-tuple-element.38), channel_id=1, source_target_pairs={{0,192},{8,200},{16,208},{24,216},{32,224},{40,232},{48,240},{56,2... | collective-permute-start | bytes 393224 | tf_op jit(solution)/shard_map/ppermute | solution.py:340

commit v2 on v1

--- a/solution.py
+++ b/solution.py
@@ -19,7 +19,7 @@
 KP = 72
 FINE = 128
 TOTAL = 16384
-VMEM = 44 * 1024 * 1024
+MIB = 1024 * 1024
 
 
 def ctx_shift(dz, dx, dc):
@@ -149,41 +149,150 @@
     out_ref[:, 1] = inverse_signal(work, inverse, twiddle, last).astype(BF)
 
 
-def inner_kernel(place_ref, weight_ref, query_ref, *refs):
-    pieces = refs[:TP]
-    inner_ref, gated_ref, keep_ref, send_ref = refs[TP:]
+def staged(kernel, scalars, ins, outs):
+    def body(*refs):
+        at = scalars + ins
+        far_in, far_out = refs[scalars:at], refs[at : at + outs]
+        at += outs
+        near_in, near_out = refs[at : at + ins], refs[at + ins : at + ins + outs]
+        sems = refs[at + ins + outs]
+        loads = [
+            pltpu.make_async_copy(far_in[i], near_in[i], sems.at[i]) for i in range(ins)
+        ]
+        for load in loads:
+            load.start()
+        for load in loads:
+            load.wait()
+        kernel(*refs[:scalars], *near_in, *near_out, *refs[at + ins + outs + 1 :])
+        stores = [
+            pltpu.make_async_copy(near_out[i], far_out[i], sems.at[ins + i]) for i in range(outs)
+        ]
+        for store in stores:
+            store.start()
+        for store in stores:
+            store.wait()
+
+    return body
+
+
+def call(kernel, outs, *args, scalars=0, scratch=(), name=None, us=3):
+    arrays = args[scalars:]
+    hbm = pl.BlockSpec(memory_space=pltpu.HBM)
+    specs = [pl.BlockSpec(memory_space=pltpu.SMEM)] * scalars + [hbm] * len(arrays)
+    return pl.pallas_call(
+        staged(kernel, scalars, len(arrays), len(outs)),
+        out_shape=[jax.ShapeDtypeStruct(shape, dtype) for shape, dtype in outs],
+        in_specs=specs,
+        out_specs=[hbm] * len(outs),
+        scratch_shapes=[pltpu.VMEM(arg.shape, arg.dtype) for arg in arrays]
+        + [pltpu.VMEM(shape, dtype) for shape, dtype in outs]
+        + [pltpu.SemaphoreType.DMA((len(arrays) + len(outs),))]
+        + list(scratch),
+        compiler_params=pltpu.CompilerParams(vmem_limit_bytes=60 * MIB),
+        cost_estimate=pl.CostEstimate(
+            flops=us * 10**9, bytes_accessed=us * 3 * 10**6, transcendentals=0
+        ),
+        name=name,
+    )(*args)
+
+
+def inner_kernel(place_ref, weight_hbm, query_hbm, *refs):
+    pieces_hbm, refs = refs[:TP], refs[TP:]
+    inner_hbm, gated_hbm, keep_hbm, send_hbm = refs[:4]
+    weight, pieces, query, inner_ref, gated_ref, load_sem, query_sem, store_sem = refs[4:]
     core = place_ref[TP]
+    loads = []
+    for idx in range(TP):
+        begin = pl.multiple_of(place_ref[idx] * 512, 512)
+        loads.append(
+            [
+                pltpu.make_async_copy(
+                    weight_hbm.at[:, pl.ds(begin, 512)], weight.at[idx], load_sem.at[2 * idx]
+                ),
+                pltpu.make_async_copy(
+                    pieces_hbm[idx], pieces.at[idx], load_sem.at[2 * idx + 1]
+                ),
+            ]
+        )
+        for load in loads[-1]:
+            load.start()
+    query_load = pltpu.make_async_copy(query_hbm, query, query_sem)
+    query_load.start()
     total = jnp.zeros((ROWS, LOC), F32)
+    stores = []
     for idx in range(TP):
-        source = place_ref[idx]
-        begin = pl.multiple_of(source * 512, 512)
-        total = total + mm(weight_ref[:, pl.ds(begin, 512)], pieces[idx][...])
+        for load in loads[idx]:
+            load.wait()
+        total = total + mm(weight[idx], pieces[idx])
         for pair in range(2):
-            slot = 2 * source + pair
+            slot = 2 * place_ref[idx] + pair
             mine = pl.multiple_of(pair * 256 + core * 128, 128)
             other = pl.multiple_of(pair * 256 + (1 - core) * 128, 128)
-            keep_ref[slot] = pieces[idx][pl.ds(mine, 128), :]
-            send_ref[slot] = pieces[idx][pl.ds(other, 128), :]
+            for where, begin, kind in ((keep_hbm, mine, 0), (send_hbm, other, 1)):
+                stores.append(
+                    pltpu.make_async_copy(
+                        pieces.at[idx, pl.ds(begin, 128)],
+                        where.at[slot],
+                        store_sem.at[4 * idx + 2 * pair + kind],
+                    )
+                )
+                stores[-1].start()
+    query_load.wait()
     inner = total.astype(BF)
     inner_ref[...] = inner
-    gated_ref[...] = (inner.astype(F32) * query_ref[...].astype(F32)).astype(BF)
+    gated_ref[...] = (inner.astype(F32) * query[...].astype(F32)).astype(BF)
+    for near, far, sem in ((inner_ref, inner_hbm, 4 * TP), (gated_ref, gated_hbm, 4 * TP + 1)):
+        stores.append(pltpu.make_async_copy(near, far, store_sem.at[sem]))
+        stores[-1].start()
+    for store in stores:
+        store.wait()
+
+
+def inner_call(place, weight_t, query, pieces):
+    hbm = pl.BlockSpec(memory_space=pltpu.HBM)
+    shapes = [(ROWS, LOC), (ROWS, LOC), (16, 128, LOC), (16, 128, LOC)]
+    return pl.pallas_call(
+        inner_kernel,
+        out_shape=[jax.ShapeDtypeStruct(shape, BF) for shape in shapes],
+        in_specs=[pl.BlockSpec(memory_space=pltpu.SMEM)] + [hbm] * (TP + 2),
+        out_specs=[hbm] * 4,
+        scratch_shapes=[
+            pltpu.VMEM((TP, ROWS, 512), BF),
+            pltpu.VMEM((TP, 512, LOC), BF),
+            pltpu.VMEM((ROWS, LOC), BF),
+            pltpu.VMEM((ROWS, LOC), BF),
+            pltpu.VMEM((ROWS, LOC), BF),
+            pltpu.SemaphoreType.DMA((2 * TP,)),
+            pltpu.SemaphoreType.DMA,
+            pltpu.SemaphoreType.DMA((4 * TP + 2,)),
+        ],
+        compiler_params=pltpu.CompilerParams(vmem_limit_bytes=60 * MIB),
+        cost_estimate=pl.CostEstimate(
+            flops=30 * 10**9, bytes_accessed=90 * 10**6, transcendentals=0
+        ),
+        name="inner",
+    )(place, weight_t, query, *pieces)
 
 
 def weight_kernel(place_ref, keep_ref, other_ref, mine_ref, sib_ref, own_ref, *outs):
     here = place_ref[0]
     for step in range(NX):
         want = lax.rem(here + step, NX)
-        for z in range(NZ):
-            slot = z * 4 + want
-            part = lax.dot_general(
-                keep_ref[slot], mine_ref[...], (((1,), (1,)), ((), ())), preferred_element_type=F32
-            ) + lax.dot_general(
-                other_ref[slot], sib_ref[...], (((1,), (1,)), ((), ())), preferred_element_type=F32
-            )
-            if step == 0:
-                own_ref[z] = part
-            else:
-                outs[step - 1][z] = part.astype(BF)
+        rows = jnp.concatenate(
+            [
+                jnp.concatenate([keep_ref[z * 4 + want], other_ref[z * 4 + want]], 1)
+                for z in range(NZ)
+            ],
+            0,
+        )
+        cols = jnp.concatenate([mine_ref[...], sib_ref[...]], 1)
+        part = lax.dot_general(
+            rows, cols, (((1,), (1,)), ((), ())), preferred_element_type=F32
+        ).reshape(NZ, 128, 512)
+        if step == 0:
+            own_ref[...] = part
+        else:
+            outs[step - 1][...] = part.astype(BF)
 
 
 def fold_kernel(place_ref, own_ref, one_ref, two_ref, three_ref, mine_ref, *outs):
@@ -235,20 +344,6 @@
         out_ref[which] = total.astype(BF)
 
 
-def call(kernel, outs, *args, scalars=0, scratch=(), name=None):
-    specs = [pl.BlockSpec(memory_space=pltpu.SMEM)] * scalars
-    specs += [pl.BlockSpec(memory_space=pltpu.VMEM)] * (len(args) - scalars)
-    return pl.pallas_call(
-        kernel,
-        out_shape=[jax.ShapeDtypeStruct(shape, dtype) for shape, dtype in outs],
-        in_specs=specs,
-        out_specs=[pl.BlockSpec(memory_space=pltpu.VMEM)] * len(outs),
-        scratch_shapes=list(scratch),
-        compiler_params=pltpu.CompilerParams(vmem_limit_bytes=VMEM),
-        name=name,
-    )(*args)
-
-
 def exchange(value):
     return lax.all_to_all(value, "ctx", split_axis=0, concat_axis=0, tiled=True)
 
@@ -260,18 +355,21 @@
     tables = [jnp.asarray(table) for table in make_tables()]
 
     far = lax.ppermute(out_cotangent, "tp", tp_shift(0, 1))
-    pieces, sources = [out_cotangent, far], [tp, y * 2 + 1 - z_hi]
-    for origin, flip in ((out_cotangent, 0), (far, 1)):
+    near = [lax.ppermute(out_cotangent, "tp", tp_shift(step, 0)) for step in (1, 3, 2)]
+    (sent,) = call(
+        prep_kernel, [((CTX, 2, CH, LOC), BF)], key_rows, value_rows, long_filter, name="prep"
+    )
+    sent, far, *near = lax.optimization_barrier((sent, far, *near))
+    pieces = [out_cotangent, far] + near
+    pieces += [lax.ppermute(far, "tp", tp_shift(step, 0)) for step in (1, 3, 2)]
+    sources = [tp, y * 2 + 1 - z_hi]
+    for flip in (0, 1):
         for step in (1, 3, 2):
-            pieces.append(lax.ppermute(origin, "tp", tp_shift(step, 0)))
             sources.append((y + 4 - step) % 4 * 2 + (z_hi + flip) % 2)
     place = jnp.stack(sources + [core]).astype(jnp.int32)
 
-    (sent,) = call(
-        prep_kernel, [((CTX, 2, CH, LOC), BF)], key_rows, value_rows, long_filter, name="prep"
-    )
+    cols = exchange(sent)
     weight_t = out_weight.T
-    cols = exchange(sent)
     spec_shape = ((CH * KP, 2 * FINE), F32)
     conv_cols, kv_spec, fil_spec = call(
         conv_kernel,
@@ -280,22 +378,15 @@
         *tables,
         scratch=[pltpu.VMEM(*spec_shape)],
         name="conv",
-    )
-    conv_out = exchange(conv_cols).reshape(ROWS, LOC)
-
-    inner, gated, keep, send = call(
-        inner_kernel,
-        [((ROWS, LOC), BF), ((ROWS, LOC), BF), ((16, 128, LOC), BF), ((16, 128, LOC), BF)],
-        place,
-        weight_t,
-        query_rows,
-        *pieces,
-        scalars=1,
-        name="inner",
-    )
+        us=30,
+    )
+    conv_cols, place = lax.optimization_barrier((conv_cols, place))
+    conv_out = exchange(conv_cols)
+    inner, gated, keep, send = inner_call(place, weight_t, query_rows, pieces)
+    conv_out, gated, send = lax.optimization_barrier((conv_out, gated, send))
+    conv_out = conv_out.reshape(ROWS, LOC)
     gated_cols = exchange(gated.reshape(CTX, CH, LOC))
     other = lax.ppermute(send, "ctx", ctx_shift(0, 0, 1))
-
     mixed = (query_rows.astype(F32) * conv_out.astype(F32)).astype(BF)
     mixed_sib = lax.ppermute(mixed, "ctx", ctx_shift(0, 0, 1))
     spot = jnp.stack([here_x, here_z]).astype(jnp.int32)
@@ -315,6 +406,7 @@
         lax.ppermute(to_x[step - 1], "ctx", ctx_shift(0, step, 0)) for step in (1, 2, 3)
     ]
 
+    gated_cols, own = lax.optimization_barrier((gated_cols, own))
     (back,) = call(
         grad_kernel,
         [((CTX, 2, CH, LOC), BF)],
@@ -324,6 +416,7 @@
         *tables,
         scratch=[pltpu.VMEM(*spec_shape), pltpu.VMEM(*spec_shape)],
         name="grad",
+        us=30,
     )
     back = exchange(back)
 
@@ -335,12 +428,12 @@
         *from_x,
         scalars=1,
         name="fold",
+        us=30,
     )
     from_z = [
         lax.ppermute(to_z[step - 1], "ctx", ctx_shift(step, 0, 0)) for step in (1, 2, 3)
     ]
-    out_weight_grad = mine + sum(value.astype(F32) for value in from_z)
-
+    back, mine = lax.optimization_barrier((back, mine))
     post, halo, filter_grad = call(
         post_kernel,
         [((3, ROWS, LOC), BF), ((ROWS, FINE), BF), ((ROWS, LOC), F32)],
@@ -355,6 +448,9 @@
     (feature_grad,) = call(
         feature_kernel, [((3, ROWS, LOC), BF)], post, halo, short_filter, name="feature"
     )
+    mine, feature_grad = lax.optimization_barrier((mine, feature_grad))
+    out_weight_grad = mine + sum(value.astype(F32) for value in from_z)
+
     return (feature_grad, filter_grad, out_weight_grad)
 
 

time: 156 us -> 144 us (0.923)
  the two profiles are of different devices: /device:TPU:39 before, /device:TPU:1 now
where the time goes in v2:
time: 144 us; the launch traced here: 143 us
  starting transfers between devices  45.9 us (32%)
  waiting for transfers between devices  44.1 us (31%)
  Pallas kernels  37.5 us (26%)
  local copies, waits for them, and re-layouts  13.5 us (9%)
    pallas_call x7, Pallas kernels, call(): pl.pallas_call(staged(kernel, scalars, len(arrays), len(outs)), out_shape...  31.4 us
    all_to_all x4, starting transfers between devices, exchange(): return lax.all_to_all(value, 'ctx', split_axis=0, concat_axis=0, tiled=True)  21.3 us
    ppermute x3, waiting for transfers between devices, local(): lax.ppermute(to_x[step - 1], 'ctx', ctx_shift(0, step, 0))  16 us
    all_to_all x4, waiting for transfers between devices, exchange(): return lax.all_to_all(value, 'ctx', split_axis=0, concat_axis=0, tiled=True)  15.6 us
    unnamed x50, local copies, waits for them, and re-layouts  12.8 us
    ppermute x3, waiting for transfers between devices, local(): lax.ppermute(out_cotangent, 'tp', tp_shift(step, 0))  8.61 us
    ppermute x1, starting transfers between devices, local(): far = lax.ppermute(out_cotangent, 'tp', tp_shift(0, 1))  7.83 us
    pallas_call x1, Pallas kernels, inner_call(): pl.pallas_call(inner_kernel, out_shape=[jax.ShapeDtypeStruct(shape, BF) f...  6.05 us
  transfers between devices with their start and end apart: 20, of which 9 were waited for; matrix products, arithmetic and copies ran while one was open for 6% of the time, Pallas kernels for 24%

profile of v2, /device:TPU:1, one launch (start us, length us, event | category | flops | bytes accessed | tf_op | source)
XLA Modules:
  0.0 143.5 jit_solution(5578706627534073151)
XLA Ops:
  0.6 7.8 %collective-permute-start = (bf16[512,256]{1,0:T(8,128)(2,1)}, bf16[512,256]{1,0:T(8,128)(2,1)S(1)}, u32[]{:S(2)}, u32[]{:S(2)}) collective-permute-start(bf16[512,256]{1,0:T(8,128)(2,1)} %refs_0_.3), channel_id=1, source_target_pairs={{0,1},{1,0},{2,3},{3,2},{4,5},{5,4},{6,7},{7,6},{8,9},{9,8},{10,11... | collective-permute-start | bytes 786440 | tf_op jit(solution)/shard_map/ppermute | solution.py:357
  8.5 1.3 collective-permute-start.1
  9.8 1.4 %collective-permute-start.2 = (bf16[512,256]{1,0:T(8,128)(2,1)}, bf16[512,256]{1,0:T(8,128)(2,1)S(1)}, u32[]{:S(2)}, u32[]{:S(2)}) collective-permute-start(bf16[512,256]{1,0:T(8,128)(2,1)} %refs_0_.3), channel_id=1, source_target_pairs={{0,6},{1,7},{2,0},{3,1},{4,2},{5,3},{6,4},{7,5},{8,14},{9,15},{10,... | collective-permute-start | bytes 786440 | tf_op jit(solution)/shard_map/ppermute | solution.py:358
  11.2 1.6 %collective-permute-start.3 = (bf16[512,256]{1,0:T(8,128)(2,1)}, bf16[512,256]{1,0:T(8,128)(2,1)S(1)}, u32[]{:S(2)}, u32[]{:S(2)}) collective-permute-start(bf16[512,256]{1,0:T(8,128)(2,1)} %refs_0_.3), channel_id=1, source_target_pairs={{0,4},{1,5},{2,6},{3,7},{4,0},{5,1},{6,2},{7,3},{8,12},{9,13},{10,... | collective-permute-start | bytes 786440 | tf_op jit(solution)/shard_map/ppermute | solution.py:358
  12.8 2.1 %prep.1 = bf16[32,2,16,256]{3,2,1,0:T(8,128)(2,1)} custom-call(bf16[512,256]{1,0:T(8,128)(2,1)} %refs_3_.3, bf16[512,256]{1,0:T(8,128)(2,1)} %refs_4_.3, f32[512,256]{1,0:T(8,128)} %refs_2_.3), custom_call_target="tpu_custom_call" | custom-call | flops 3000000000 | bytes 9000000 | tf_op jit(solution)/shard_map/prep/pallas_call | solution.py:182
  15.0 0.0 copy-start.12
  15.0 2.0 %collective-permute-done.1.refs_2_ = bf16[512,256]{1,0:T(8,128)(2,1)S(1)} collective-permute-done((bf16[512,256]{1,0:T(8,128)(2,1)}, bf16[512,256]{1,0:T(8,128)(2,1)S(1)}, u32[]{:S(2)}, u32[]{:S(2)}) %collective-permute-start.1) | collective-permute-done | bytes 262176 | tf_op jit(solution)/shard_map/ppermute | solution.py:358
  16.9 0.0 collective-permute-done.2.refs_3_
  16.9 6.7 %collective-permute-done.3.refs_4_ = bf16[512,256]{1,0:T(8,128)(2,1)S(1)} collective-permute-done((bf16[512,256]{1,0:T(8,128)(2,1)}, bf16[512,256]{1,0:T(8,128)(2,1)S(1)}, u32[]{:S(2)}, u32[]{:S(2)}) %collective-permute-start.3) | collective-permute-done | bytes 262176 | tf_op jit(solution)/shard_map/ppermute | solution.py:358
  23.6 7.7 %all-to-all-start = ((bf16[32,2,16,256]{3,2,1,0:T(8,128)(2,1)}), bf16[32,2,16,256]{3,2,1,0:T(8,128)(2,1)S(1)}, u32[]{:S(2)}, u32[]{:S(2)}) async-start(bf16[32,2,16,256]{3,2,1,0:T(8,128)(2,1)} %prep.1), calls=%async_computation | async-start | bytes 1048576 | tf_op jit(solution)/shard_map/all_to_all | solution.py:348
  31.4 6.4 %copy.15 = bf16[4096,512]{0,1:T(8,128)(2,1)} copy(bf16[4096,512]{1,0:T(8,128)(2,1)} %param.18) | data formatting | bytes 8388608 | tf_op args[6]
  37.8 0.7 stack.48.place_ref
  38.5 0.9 collective-permute-start.4
  39.4 1.8 %collective-permute-start.5 = (bf16[512,256]{1,0:T(8,128)(2,1)S(1)}, bf16[512,256]{1,0:T(8,128)(2,1)S(1)}, u32[]{:S(2)}, u32[]{:S(2)}) collective-permute-start(bf16[512,256]{1,0:T(8,128)(2,1)S(1)} %collective-permute-done.refs_1_), channel_id=1, source_target_pairs={{0,6},{1,7},{2,0},{3,1},{4,2},{5,3},{6,4},{7,5},{8,14},{9,15},{10,... | collective-permute-start | bytes 786440 | tf_op jit(solution)/shard_map/ppermute | solution.py:364
  41.2 0.0 collective-permute-start.6
  41.2 6.5 %all-to-all-done.refs_0_ = bf16[32,2,16,256]{3,2,1,0:T(8,128)(2,1)S(1)} async-done(((bf16[32,2,16,256]{3,2,1,0:T(8,128)(2,1)}), bf16[32,2,16,256]{3,2,1,0:T(8,128)(2,1)S(1)}, u32[]{:S(2)}, u32[]{:S(2)}) %all-to-all-start) | async-done | bytes 524320 | tf_op jit(solution)/shard_map/all_to_all | solution.py:348
  47.7 0.8 copy-done.1
  48.5 5.8 %conv.1 = (bf16[32,16,256]{2,1,0:T(8,128)(2,1)}, f32[1152,256]{1,0:T(8,128)}, f32[1152,256]{1,0:T(8,128)}) custom-call(bf16[32,2,16,256]{3,2,1,0:T(8,128)(2,1)} %copy-done.1, bf16[144,128]{1,0:T(8,128)(2,1)} %constant.116.clone.refs_1_.refs_3_, bf16[2,256,256]{2,1,0:T(8,128)(2,1)} %constant.117.clone.refs_2_.refs_4_, ...), custom_call_target="tpu_custom_call" | custom-call | flops 30000001024 | bytes 90000000 | tf_op jit(solution)/shard_map/conv/pallas_call | solution.py:182
  54.3 4.2 %all-to-all-start.1 = ((bf16[32,16,256]{2,1,0:T(8,128)(2,1)}), bf16[32,16,256]{2,1,0:T(8,128)(2,1)S(1)}, u32[]{:S(2)}, u32[]{:S(2)}) async-start(bf16[32,16,256]{2,1,0:T(8,128)(2,1)} %get-tuple-element.39), calls=%async_computation.1 | async-start | bytes 524288 | tf_op jit(solution)/shard_map/all_to_all | solution.py:348
  58.5 0.0 copy-start.17
  58.5 0.0 collective-permute-done.5.refs_6_
  58.5 0.0 collective-permute-done.6.refs_7_
  58.5 0.7 copy-done.17
  59.2 0.1 copy-done.18
  59.2 0.1 copy-done.19
  59.3 6.1 %inner.1 = (bf16[512,256]{1,0:T(8,128)(2,1)}, bf16[512,256]{1,0:T(8,128)(2,1)}, bf16[16,128,256]{2,1,0:T(8,128)(2,1)}, bf16[16,128,256]{2,1,0:T(8,128)(2,1)}) custom-call(s32[9]{0:T(128)} %stack.48.place_ref, bf16[512,4096]{1,0:T(8,128)(2,1)} %bitcast.15, bf16[512,256]{1,0:T(8,128)(2,1)} %query_hbm.1, bf16[512,256]{1,0:T(8,128)(2,1)} %refs_0_.3, ...), custom_call_target="tpu_custom_call" | custom-call | flops 30000001024 | bytes 90000000 | tf_op jit(solution)/shard_map/inner/pallas_call | solution.py:254
  65.4 4.1 %all-to-all-done.1 = bf16[32,16,256]{2,1,0:T(8,128)(2,1)S(1)} async-done(((bf16[32,16,256]{2,1,0:T(8,128)(2,1)}), bf16[32,16,256]{2,1,0:T(8,128)(2,1)S(1)}, u32[]{:S(2)}, u32[]{:S(2)}) %all-to-all-start.1) | async-done | bytes 262176 | tf_op jit(solution)/shard_map/all_to_all | solution.py:348
  69.5 0.2 collective-permute-start.7
  69.8 0.1 multiply_convert_fusion.refs_3_
  69.9 0.0 copy-start.4
  69.9 0.4 collective-permute-start.8
  70.2 3.8 %all-to-all-start.2 = ((bf16[32,16,256]{2,1,0:T(8,128)(2,1)}), bf16[32,16,256]{2,1,0:T(8,128)(2,1)S(1)}, u32[]{:S(2)}, u32[]{:S(2)}) async-start(bf16[32,16,256]{2,1,0:T(8,128)(2,1)} %bitcast.17), calls=%async_computation.2 | async-start | bytes 524288 | tf_op jit(solution)/shard_map/all_to_all | solution.py:348
  74.1 0.6 pad_add_fusion.refs_0_
  74.8 0.7 copy-done.16
  75.4 0.4 copy-done.8
  75.8 4.5 %weight.1 = (f32[4,128,512]{2,1,0:T(8,128)}, bf16[4,128,512]{2,1,0:T(8,128)(2,1)}, bf16[4,128,512]{2,1,0:T(8,128)(2,1)}, bf16[4,128,512]{2,1,0:T(8,128)(2,1)}) custom-call(s32[2]{0:T(128)} %pad_add_fusion.refs_0_, bf16[16,128,256]{2,1,0:T(8,128)(2,1)} %get-tuple-element.48.refs_1_, bf16[16,128,256]{2,1,0:T(8,128)(2,1)} %copy-done.8, ...), custom_call_target="tpu_custom_call" | custom-call | flops 3000000000 | bytes 9000000 | tf_op jit(solution)/shard_map/weight/pallas_call | solution.py:182
  80.3 4.9 %all-to-all-done.2.refs_0_ = bf16[32,16,256]{2,1,0:T(8,128)(2,1)S(1)} async-done(((bf16[32,16,256]{2,1,0:T(8,128)(2,1)}), bf16[32,16,256]{2,1,0:T(8,128)(2,1)S(1)}, u32[]{:S(2)}, u32[]{:S(2)}) %all-to-all-start.2) | async-done | bytes 262176 | tf_op jit(solution)/shard_map/all_to_all | solution.py:348
  85.2 0.4 collective-permute-start.9
  85.6 1.8 %collective-permute-start.10 = (bf16[4,128,512]{2,1,0:T(8,128)(2,1)}, bf16[4,128,512]{2,1,0:T(8,128)(2,1)S(1)}, u32[]{:S(2)}, u32[]{:S(2)}) collective-permute-start(bf16[4,128,512]{2,1,0:T(8,128)(2,1)} %get-tuple-element.57), channel_id=1, source_target_pairs={{0,32},{8,40},{16,48},{24,56},{32,0},{40,8},{48,16},{56,24},{64,96... | collective-permute-start | bytes 1572872 | tf_op jit(solution)/shard_map/ppermute | solution.py:406
  87.5 0.5 collective-permute-start.11
  88.0 6.0 %grad.1 = bf16[32,2,16,256]{3,2,1,0:T(8,128)(2,1)} custom-call(bf16[32,16,256]{2,1,0:T(8,128)(2,1)} %copy-done.6, f32[1152,256]{1,0:T(8,128)} %get-tuple-element.53.refs_1_, f32[1152,256]{1,0:T(8,128)} %get-tuple-element.54.refs_2_, bf16[144,128]{1,0:T(8,128)(2,1)} %constant.116.clone.refs_1_.refs_3_, bf16[2,256,256]{2,1,0:T(8,128)(2,1)} %constant.117.clone.refs_2_.refs_4_, ...), custom_call_target="tpu_custom_call" | custom-call | flops 30000001024 | bytes 90000000 | tf_op jit(solution)/shard_map/grad/pallas_call | solution.py:182
  94.1 5.6 %all-to-all-start.3 = ((bf16[32,2,16,256]{3,2,1,0:T(8,128)(2,1)}), bf16[32,2,16,256]{3,2,1,0:T(8,128)(2,1)S(1)}, u32[]{:S(2)}, u32[]{:S(2)}) async-start(bf16[32,2,16,256]{3,2,1,0:T(8,128)(2,1)} %grad.1), calls=%async_computation.3 | async-start | bytes 1048576 | tf_op jit(solution)/shard_map/all_to_all | solution.py:348
  99.7 0.3 collective-permute-done.9.refs_2_
  100.0 15.1 %collective-permute-done.10.refs_3_ = bf16[4,128,512]{2,1,0:T(8,128)(2,1)S(1)} collective-permute-done((bf16[4,128,512]{2,1,0:T(8,128)(2,1)}, bf16[4,128,512]{2,1,0:T(8,128)(2,1)S(1)}, u32[]{:S(2)}, u32[]{:S(2)}) %collective-permute-start.10) | collective-permute-done | bytes 524320 | tf_op jit(solution)/shard_map/ppermute | solution.py:406
  115.1 0.6 collective-permute-done.11.refs_4_
  115.7 0.2 copy-done.10
  115.9 0.8 copy-done.11
  116.7 3.3 %fold.1 = (f32[128,512]{1,0:T(8,128)}, bf16[128,512]{1,0:T(8,128)(2,1)}, bf16[128,512]{1,0:T(8,128)(2,1)}, bf16[128,512]{1,0:T(8,128)(2,1)}) custom-call(s32[2]{0:T(128)} %pad_add_fusion.refs_0_, f32[4,128,512]{2,1,0:T(8,128)} %get-tuple-element.55.refs_1_, bf16[4,128,512]{2,1,0:T(8,128)(2,1)} %copy-done.9, bf16[4,128,512]{2,1,0:T(8,128)(2,1)} %copy-done.10, ...), custom_call_target="tpu_custom_call" | custom-call | flops 30000001024 | bytes 90000000 | tf_op jit(solution)/shard_map/fold/pallas_call | solution.py:182
  120.0 0.0 all-to-all-done.3.refs_0_
  120.0 0.0 copy-start.2
  120.0 0.8 copy-done.2
  120.8 2.8 %post.1 = (bf16[3,512,256]{2,1,0:T(8,128)(2,1)}, bf16[512,128]{1,0:T(8,128)(2,1)}, f32[512,256]{1,0:T(8,128)}) custom-call(bf16[32,2,16,256]{3,2,1,0:T(8,128)(2,1)} %copy-done.2, bf16[512,256]{1,0:T(8,128)(2,1)} %get-tuple-element.62.refs_1_, bf16[512,256]{1,0:T(8,128)(2,1)} %bitcast.16, bf16[512,256]{1,0:T(8,128)(2,1)} %refs_3_.3, bf16[512,256]{1,0:T(8,128)(2,1)} %refs_4_.3), custom_call_target="tpu_custom_call" | custom-call | flops 3000000000 | bytes 9000000 | tf_op jit(solution)/shard_map/post/pallas_call | solution.py:182
  123.6 4.4 %collective-permute-start.12 = (bf16[512,128]{1,0:T(8,128)(2,1)}, bf16[512,128]{1,0:T(8,128)(2,1)S(1)}, u32[]{:S(2)}, u32[]{:S(2)}) collective-permute-start(bf16[512,128]{1,0:T(8,128)(2,1)} %get-tuple-element.64), channel_id=1, source_target_pairs={{8,0},{16,8},{24,16},{32,24},{40,32},{48,40},{56,48},{64,56},{72,6... | collective-permute-start | bytes 393224 | tf_op jit(solution)/shard_map/ppermute | solution.py:447
  128.0 1.2 copy.16.refs_2_
  129.2 1.3 collective-permute-start.15
  130.5 0.5 collective-permute-start.14
  130.9 0.2 collective-permute-start.13
  131.2 0.0 collective-permute-done.12.refs_1_
  131.2 0.6 copy-done.23
  131.8 7.0 %feature.1 = bf16[3,512,256]{2,1,0:T(8,128)(2,1)} custom-call(bf16[3,512,256]{2,1,0:T(8,128)(2,1)} %get-tuple-element.63.refs_0_, bf16[512,128]{1,0:T(8,128)(2,1)} %copy-done.23, f32[3,512,7]{2,1,0:T(8,128)} %copy.16.refs_2_), custom_call_target="tpu_custom_call" | custom-call | flops 3000000000 | bytes 9000000 | tf_op jit(solution)/shard_map/feature/pallas_call | solution.py:182
  138.8 0.0 collective-permute-done.15
  138.8 3.9 %collective-permute-done.14 = bf16[128,512]{1,0:T(8,128)(2,1)S(1)} collective-permute-done((bf16[128,512]{1,0:T(8,128)(2,1)S(1)}, bf16[128,512]{1,0:T(8,128)(2,1)S(1)}, u32[]{:S(2)}, u32[]{:S(2)}) %collective-permute-start.14) | collective-permute-done | bytes 131104 | tf_op jit(solution)/shard_map/ppermute | solution.py:434
  142.7 0.0 collective-permute-done.13
  142.7 0.8 add_add_fusion
  (38 shorter events, 0.1 us)
Async XLA Ops:
  0.6 14.3 %collective-permute-start = (bf16[512,256]{1,0:T(8,128)(2,1)}, bf16[512,256]{1,0:T(8,128)(2,1)S(1)}, u32[]{:S(2)}, u32[]{:S(2)}) collective-permute-start(bf16[512,256]{1,0:T(8,128)(2,1)} %refs_0_.3), channel_id=1, source_target_pairs={{0,1},{1,0},{2,3},{3,2},{4,5},{5,4},{6,7},{7,6},{8,9},{9,8},{10,11... | collective-permute-start | bytes 786440 | tf_op jit(solution)/shard_map/ppermute | solution.py:357
  8.5 8.5 %collective-permute-start.1 = (bf16[512,256]{1,0:T(8,128)(2,1)}, bf16[512,256]{1,0:T(8,128)(2,1)S(1)}, u32[]{:S(2)}, u32[]{:S(2)}) collective-permute-start(bf16[512,256]{1,0:T(8,128)(2,1)} %refs_0_.3), channel_id=1, source_target_pairs={{0,2},{1,3},{2,4},{3,5},{4,6},{5,7},{6,0},{7,1},{8,10},{9,11},{10,... | collective-permute-start | bytes 786440 | tf_op jit(solution)/shard_map/ppermute | solution.py:358
  9.8 7.2 %collective-permute-start.2 = (bf16[512,256]{1,0:T(8,128)(2,1)}, bf16[512,256]{1,0:T(8,128)(2,1)S(1)}, u32[]{:S(2)}, u32[]{:S(2)}) collective-permute-start(bf16[512,256]{1,0:T(8,128)(2,1)} %refs_0_.3), channel_id=1, source_target_pairs={{0,6},{1,7},{2,0},{3,1},{4,2},{5,3},{6,4},{7,5},{8,14},{9,15},{10,... | collective-permute-start | bytes 786440 | tf_op jit(solution)/shard_map/ppermute | solution.py:358
  11.2 12.4 %collective-permute-start.3 = (bf16[512,256]{1,0:T(8,128)(2,1)}, bf16[512,256]{1,0:T(8,128)(2,1)S(1)}, u32[]{:S(2)}, u32[]{:S(2)}) collective-permute-start(bf16[512,256]{1,0:T(8,128)(2,1)} %refs_0_.3), channel_id=1, source_target_pairs={{0,4},{1,5},{2,6},{3,7},{4,0},{5,1},{6,2},{7,3},{8,12},{9,13},{10,... | collective-permute-start | bytes 786440 | tf_op jit(solution)/shard_map/ppermute | solution.py:358
  15.0 26.2 %copy-start.12 = (bf16[512,256]{1,0:T(8,128)(2,1)}, bf16[512,256]{1,0:T(8,128)(2,1)S(1)}, u32[]{:S(2)}) copy-start(bf16[512,256]{1,0:T(8,128)(2,1)S(1)} %collective-permute-done.refs_1_) | copy-start | bytes 786436
  16.9 20.9 %copy-start.13 = (bf16[512,256]{1,0:T(8,128)(2,1)}, bf16[512,256]{1,0:T(8,128)(2,1)S(1)}, u32[]{:S(2)}) copy-start(bf16[512,256]{1,0:T(8,128)(2,1)S(1)} %collective-permute-done.1.refs_2_) | copy-start | bytes 786436
  16.9 20.9 %copy-start.14 = (bf16[512,256]{1,0:T(8,128)(2,1)}, bf16[512,256]{1,0:T(8,128)(2,1)S(1)}, u32[]{:S(2)}) copy-start(bf16[512,256]{1,0:T(8,128)(2,1)S(1)} %collective-permute-done.2.refs_3_) | copy-start | bytes 786436
  23.6 14.2 %copy-start.15 = (bf16[512,256]{1,0:T(8,128)(2,1)}, bf16[512,256]{1,0:T(8,128)(2,1)S(1)}, u32[]{:S(2)}) copy-start(bf16[512,256]{1,0:T(8,128)(2,1)S(1)} %collective-permute-done.3.refs_4_) | copy-start | bytes 786436
  23.6 24.1 %all-to-all-start = ((bf16[32,2,16,256]{3,2,1,0:T(8,128)(2,1)}), bf16[32,2,16,256]{3,2,1,0:T(8,128)(2,1)S(1)}, u32[]{:S(2)}, u32[]{:S(2)}) async-start(bf16[32,2,16,256]{3,2,1,0:T(8,128)(2,1)} %prep.1), calls=%async_computation | async-start | bytes 1048576 | tf_op jit(solution)/shard_map/all_to_all | solution.py:348
  38.5 19.9 %collective-permute-start.4 = (bf16[512,256]{1,0:T(8,128)(2,1)S(1)}, bf16[512,256]{1,0:T(8,128)(2,1)S(1)}, u32[]{:S(2)}, u32[]{:S(2)}) collective-permute-start(bf16[512,256]{1,0:T(8,128)(2,1)S(1)} %collective-permute-done.refs_1_), channel_id=1, source_target_pairs={{0,2},{1,3},{2,4},{3,5},{4,6},{5,7},{6,0},{7,1},{8,10},{9,11},{10,... | collective-permute-start | bytes 786440 | tf_op jit(solution)/shard_map/ppermute | solution.py:364
  39.4 19.1 %collective-permute-start.5 = (bf16[512,256]{1,0:T(8,128)(2,1)S(1)}, bf16[512,256]{1,0:T(8,128)(2,1)S(1)}, u32[]{:S(2)}, u32[]{:S(2)}) collective-permute-start(bf16[512,256]{1,0:T(8,128)(2,1)S(1)} %collective-permute-done.refs_1_), channel_id=1, source_target_pairs={{0,6},{1,7},{2,0},{3,1},{4,2},{5,3},{6,4},{7,5},{8,14},{9,15},{10,... | collective-permute-start | bytes 786440 | tf_op jit(solution)/shard_map/ppermute | solution.py:364
  41.2 17.3 %collective-permute-start.6 = (bf16[512,256]{1,0:T(8,128)(2,1)S(1)}, bf16[512,256]{1,0:T(8,128)(2,1)S(1)}, u32[]{:S(2)}, u32[]{:S(2)}) collective-permute-start(bf16[512,256]{1,0:T(8,128)(2,1)S(1)} %collective-permute-done.refs_1_), channel_id=1, source_target_pairs={{0,4},{1,5},{2,6},{3,7},{4,0},{5,1},{6,2},{7,3},{8,12},{9,13},{10,... | collective-permute-start | bytes 786440 | tf_op jit(solution)/shard_map/ppermute | solution.py:364
  47.7 0.8 copy-start.1
  54.3 15.3 %all-to-all-start.1 = ((bf16[32,16,256]{2,1,0:T(8,128)(2,1)}), bf16[32,16,256]{2,1,0:T(8,128)(2,1)S(1)}, u32[]{:S(2)}, u32[]{:S(2)}) async-start(bf16[32,16,256]{2,1,0:T(8,128)(2,1)} %get-tuple-element.39), calls=%async_computation.1 | async-start | bytes 524288 | tf_op jit(solution)/shard_map/all_to_all | solution.py:348
  58.5 0.7 copy-start.17
  58.5 0.8 copy-start.18
  58.5 0.8 copy-start.19
  59.3 10.4 %copy-start.3 = (bf16[512,256]{1,0:T(8,128)(2,1)S(1)}, bf16[512,256]{1,0:T(8,128)(2,1)}, u32[]{:S(2)}) copy-start(bf16[512,256]{1,0:T(8,128)(2,1)} %query_hbm.1) | copy-start | bytes 786436
  69.5 10.7 %copy-start = (bf16[32,16,256]{2,1,0:T(8,128)(2,1)}, bf16[32,16,256]{2,1,0:T(8,128)(2,1)S(1)}, u32[]{:S(2)}) copy-start(bf16[32,16,256]{2,1,0:T(8,128)(2,1)S(1)} %all-to-all-done.1) | copy-start | bytes 786436
  69.5 5.2 %collective-permute-start.7 = (bf16[16,128,256]{2,1,0:T(8,128)(2,1)}, bf16[16,128,256]{2,1,0:T(8,128)(2,1)S(1)}, u32[]{:S(2)}, u32[]{:S(2)}) collective-permute-start(bf16[16,128,256]{2,1,0:T(8,128)(2,1)} %get-tuple-element.49), channel_id=1, source_target_pairs={{0,8},{8,0},{16,24},{24,16},{32,40},{40,32},{48,56},{56,48},{64,72... | collective-permute-start | bytes 3145736 | tf_op jit(solution)/shard_map/ppermute | solution.py:389
  69.9 4.9 %copy-start.4 = (bf16[512,256]{1,0:T(8,128)(2,1)}, bf16[512,256]{1,0:T(8,128)(2,1)S(1)}, u32[]{:S(2)}) copy-start(bf16[512,256]{1,0:T(8,128)(2,1)S(1)} %multiply_convert_fusion.refs_3_) | copy-start | bytes 786436
  69.9 4.8 %collective-permute-start.8 = (bf16[512,256]{1,0:T(8,128)(2,1)S(1)}, bf16[512,256]{1,0:T(8,128)(2,1)S(1)}, u32[]{:S(2)}, u32[]{:S(2)}) collective-permute-start(bf16[512,256]{1,0:T(8,128)(2,1)S(1)} %multiply_convert_fusion.refs_3_), channel_id=1, source_target_pairs={{0,8},{8,0},{16,24},{24,16},{32,40},{40,32},{48,56},{56,48},{64,72... | collective-permute-start | bytes 786440 | tf_op jit(solution)/shard_map/ppermute | solution.py:391
  70.2 15.0 %all-to-all-start.2 = ((bf16[32,16,256]{2,1,0:T(8,128)(2,1)}), bf16[32,16,256]{2,1,0:T(8,128)(2,1)S(1)}, u32[]{:S(2)}, u32[]{:S(2)}) async-start(bf16[32,16,256]{2,1,0:T(8,128)(2,1)} %bitcast.17), calls=%async_computation.2 | async-start | bytes 524288 | tf_op jit(solution)/shard_map/all_to_all | solution.py:348
  74.7 0.7 copy-start.16
  74.7 1.1 copy-start.8
  85.2 2.8 %copy-start.6 = (bf16[32,16,256]{2,1,0:T(8,128)(2,1)}, bf16[32,16,256]{2,1,0:T(8,128)(2,1)S(1)}, u32[]{:S(2)}) copy-start(bf16[32,16,256]{2,1,0:T(8,128)(2,1)S(1)} %all-to-all-done.2.refs_0_) | copy-start | bytes 786436
  85.2 14.8 %collective-permute-start.9 = (bf16[4,128,512]{2,1,0:T(8,128)(2,1)}, bf16[4,128,512]{2,1,0:T(8,128)(2,1)S(1)}, u32[]{:S(2)}, u32[]{:S(2)}) collective-permute-start(bf16[4,128,512]{2,1,0:T(8,128)(2,1)} %get-tuple-element.56), channel_id=1, source_target_pairs={{0,16},{8,24},{16,32},{24,40},{32,48},{40,56},{48,0},{56,8},{64,80... | collective-permute-start | bytes 1572872 | tf_op jit(solution)/shard_map/ppermute | solution.py:406
  85.6 29.5 %collective-permute-start.10 = (bf16[4,128,512]{2,1,0:T(8,128)(2,1)}, bf16[4,128,512]{2,1,0:T(8,128)(2,1)S(1)}, u32[]{:S(2)}, u32[]{:S(2)}) collective-permute-start(bf16[4,128,512]{2,1,0:T(8,128)(2,1)} %get-tuple-element.57), channel_id=1, source_target_pairs={{0,32},{8,40},{16,48},{24,56},{32,0},{40,8},{48,16},{56,24},{64,96... | collective-permute-start | bytes 1572872 | tf_op jit(solution)/shard_map/ppermute | solution.py:406
  87.5 28.2 %collective-permute-start.11 = (bf16[4,128,512]{2,1,0:T(8,128)(2,1)}, bf16[4,128,512]{2,1,0:T(8,128)(2,1)S(1)}, u32[]{:S(2)}, u32[]{:S(2)}) collective-permute-start(bf16[4,128,512]{2,1,0:T(8,128)(2,1)} %get-tuple-element.58), channel_id=1, source_target_pairs={{0,48},{8,56},{16,0},{24,8},{32,16},{40,24},{48,32},{56,40},{64,11... | collective-permute-start | bytes 1572872 | tf_op jit(solution)/shard_map/ppermute | solution.py:406
  94.1 26.0 %all-to-all-start.3 = ((bf16[32,2,16,256]{3,2,1,0:T(8,128)(2,1)}), bf16[32,2,16,256]{3,2,1,0:T(8,128)(2,1)S(1)}, u32[]{:S(2)}, u32[]{:S(2)}) async-start(bf16[32,2,16,256]{3,2,1,0:T(8,128)(2,1)} %grad.1), calls=%async_computation.3 | async-start | bytes 1048576 | tf_op jit(solution)/shard_map/all_to_all | solution.py:348
  100.0 15.7 %copy-start.9 = (bf16[4,128,512]{2,1,0:T(8,128)(2,1)}, bf16[4,128,512]{2,1,0:T(8,128)(2,1)S(1)}, u32[]{:S(2)}) copy-start(bf16[4,128,512]{2,1,0:T(8,128)(2,1)S(1)} %collective-permute-done.9.refs_2_) | copy-start | bytes 1572868
  115.1 0.8 copy-start.10
  115.9 0.8 copy-start.11
  120.0 0.8 copy-start.2
  120.8 7.2 %copy-start.7 = (f32[3,512,7]{1,2,0:T(8,128)S(1)}, f32[3,512,7]{1,2,0:T(8,128)}, u32[]{:S(2)}) copy-start(f32[3,512,7]{1,2,0:T(8,128)} %param.17) | copy-start | bytes 129028
  120.8 8.4 %copy-start.22 = (bf16[128,512]{1,0:T(8,128)(2,1)S(1)}, bf16[128,512]{1,0:T(8,128)(2,1)}, u32[]{:S(2)}) copy-start(bf16[128,512]{1,0:T(8,128)(2,1)} %get-tuple-element.70) | copy-start | bytes 393220
  120.8 9.6 %copy-start.21 = (bf16[128,512]{1,0:T(8,128)(2,1)S(1)}, bf16[128,512]{1,0:T(8,128)(2,1)}, u32[]{:S(2)}) copy-start(bf16[128,512]{1,0:T(8,128)(2,1)} %get-tuple-element.69) | copy-start | bytes 393220
  120.8 10.1 %copy-start.20 = (bf16[128,512]{1,0:T(8,128)(2,1)S(1)}, bf16[128,512]{1,0:T(8,128)(2,1)}, u32[]{:S(2)}) copy-start(bf16[128,512]{1,0:T(8,128)(2,1)} %get-tuple-element.68) | copy-start | bytes 393220
  123.6 7.6 %collective-permute-start.12 = (bf16[512,128]{1,0:T(8,128)(2,1)}, bf16[512,128]{1,0:T(8,128)(2,1)S(1)}, u32[]{:S(2)}, u32[]{:S(2)}) collective-permute-start(bf16[512,128]{1,0:T(8,128)(2,1)} %get-tuple-element.64), channel_id=1, source_target_pairs={{8,0},{16,8},{24,16},{32,24},{40,32},{48,40},{56,48},{64,56},{72,6... | collective-permute-start | bytes 393224 | tf_op jit(solution)/shard_map/ppermute | solution.py:447
  129.2 9.6 %collective-permute-start.15 = (bf16[128,512]{1,0:T(8,128)(2,1)S(1)}, bf16[128,512]{1,0:T(8,128)(2,1)S(1)}, u32[]{:S(2)}, u32[]{:S(2)}) collective-permute-start(bf16[128,512]{1,0:T(8,128)(2,1)S(1)} %copy-done.22), channel_id=1, source_target_pairs={{0,192},{8,200},{16,208},{24,216},{32,224},{40,232},{48,240},{56,2... | collective-permute-start | bytes 393224 | tf_op jit(solution)/shard_map/ppermute | solution.py:434
  130.5 12.2 %collective-permute-start.14 = (bf16[128,512]{1,0:T(8,128)(2,1)S(1)}, bf16[128,512]{1,0:T(8,128)(2,1)S(1)}, u32[]{:S(2)}, u32[]{:S(2)}) collective-permute-start(bf16[128,512]{1,0:T(8,128)(2,1)S(1)} %copy-done.21), channel_id=1, source_target_pairs={{0,128},{8,136},{16,144},{24,152},{32,160},{40,168},{48,176},{56,1... | collective-permute-start | bytes 393224 | tf_op jit(solution)/shard_map/ppermute | solution.py:434
  130.9 11.8 %collective-permute-start.13 = (bf16[128,512]{1,0:T(8,128)(2,1)S(1)}, bf16[128,512]{1,0:T(8,128)(2,1)S(1)}, u32[]{:S(2)}, u32[]{:S(2)}) collective-permute-start(bf16[128,512]{1,0:T(8,128)(2,1)S(1)} %copy-done.20), channel_id=1, source_target_pairs={{0,64},{8,72},{16,80},{24,88},{32,96},{40,104},{48,112},{56,120},{... | collective-permute-start | bytes 393224 | tf_op jit(solution)/shard_map/ppermute | solution.py:434
  131.2 0.6 copy-start.23
  131.8 10.9 %copy-start.5 = (f32[128,512]{1,0:T(8,128)S(1)}, f32[128,512]{1,0:T(8,128)}, u32[]{:S(2)}) copy-start(f32[128,512]{1,0:T(8,128)} %get-tuple-element.67) | copy-start | bytes 786436

commit v3 on v2

--- a/solution.py
+++ b/solution.py
@@ -336,7 +336,7 @@
     for which in range(3):
         tail = halo if which == 0 else pltpu.roll(halo, FINE - 8 * which, 1)
         wide = jnp.concatenate([post_ref[which].astype(F32), tail], 1)
-        taps = taps_ref[which]
+        taps = jnp.concatenate([taps_ref[which], jnp.zeros((1, ROWS), F32)], 0).T
         total = taps[:, 0:1] * wide[:, :LOC]
         for offset in range(1, 7):
             moved = pltpu.roll(wide, LOC + FINE - offset, 1)
@@ -416,7 +416,7 @@
         *tables,
         scratch=[pltpu.VMEM(*spec_shape), pltpu.VMEM(*spec_shape)],
         name="grad",
-        us=30,
+        us=5,
     )
     back = exchange(back)
 
@@ -446,7 +446,7 @@
     )
     halo = lax.ppermute(halo, "ctx", [(source, source - 1) for source in range(1, CTX)])
     (feature_grad,) = call(
-        feature_kernel, [((3, ROWS, LOC), BF)], post, halo, short_filter, name="feature"
+        feature_kernel, [((3, ROWS, LOC), BF)], post, halo, short_filter.transpose(0, 2, 1), name="feature"
     )
     mine, feature_grad = lax.optimization_barrier((mine, feature_grad))
     out_weight_grad = mine + sum(value.astype(F32) for value in from_z)

time: 144 us -> 140 us (0.972)
  the two profiles are of different devices: /device:TPU:1 before, /device:TPU:39 now
where the time goes in v3:
time: 140 us
  starting transfers between devices  53.7 us (38%)
  Pallas kernels  37.1 us (26%)
  waiting for transfers between devices  33.5 us (24%)
  local copies, waits for them, and re-layouts  12.8 us (9%)
  other arithmetic  1.51 us (1%)
    pallas_call x7, Pallas kernels, call(): pl.pallas_call(staged(kernel, scalars, len(arrays), len(outs)), out_shape...  31.1 us
    all_to_all x4, starting transfers between devices, exchange(): return lax.all_to_all(value, 'ctx', split_axis=0, concat_axis=0, tiled=True)  30.3 us
    ppermute x3, waiting for transfers between devices, local(): lax.ppermute(to_x[step - 1], 'ctx', ctx_shift(0, step, 0))  13.8 us
    unnamed x47, local copies, waits for them, and re-layouts  12.1 us
    ppermute x1, waiting for transfers between devices, local(): lax.ppermute(halo, 'ctx', [(source, source - 1) for source in range(1, CT...  7.9 us
    ppermute x1, waiting for transfers between devices, local(): far = lax.ppermute(out_cotangent, 'tp', tp_shift(0, 1))  7.8 us
    pallas_call x1, Pallas kernels, inner_call(): pl.pallas_call(inner_kernel, out_shape=[jax.ShapeDtypeStruct(shape, BF) f...  6.06 us
    ppermute x1, starting transfers between devices, local(): far = lax.ppermute(out_cotangent, 'tp', tp_shift(0, 1))  6.01 us
  transfers between devices with their start and end apart: 20, of which 5 were waited for; matrix products, arithmetic and copies ran while one was open for 6% of the time, Pallas kernels for 25%

profile of v3, /device:TPU:39, one launch (start us, length us, event | category | flops | bytes accessed | tf_op | source)
XLA Modules:
  0.0 139.7 jit_solution(808645542853341431)
XLA Ops:
  0.6 2.8 %collective-permute-start.2 = (bf16[512,256]{1,0:T(8,128)(2,1)}, bf16[512,256]{1,0:T(8,128)(2,1)S(1)}, u32[]{:S(2)}, u32[]{:S(2)}) collective-permute-start(bf16[512,256]{1,0:T(8,128)(2,1)} %refs_0_.3), channel_id=1, source_target_pairs={{0,6},{1,7},{2,0},{3,1},{4,2},{5,3},{6,4},{7,5},{8,14},{9,15},{10,... | collective-permute-start | bytes 786440 | tf_op jit(solution)/shard_map/ppermute | solution.py:358
  3.4 0.0 collective-permute-start.1
  3.4 6.0 %collective-permute-start = (bf16[512,256]{1,0:T(8,128)(2,1)}, bf16[512,256]{1,0:T(8,128)(2,1)S(1)}, u32[]{:S(2)}, u32[]{:S(2)}) collective-permute-start(bf16[512,256]{1,0:T(8,128)(2,1)} %refs_0_.3), channel_id=1, source_target_pairs={{0,1},{1,0},{2,3},{3,2},{4,5},{5,4},{6,7},{7,6},{8,9},{9,8},{10,11... | collective-permute-start | bytes 786440 | tf_op jit(solution)/shard_map/ppermute | solution.py:357
  9.5 1.6 %collective-permute-start.3 = (bf16[512,256]{1,0:T(8,128)(2,1)}, bf16[512,256]{1,0:T(8,128)(2,1)S(1)}, u32[]{:S(2)}, u32[]{:S(2)}) collective-permute-start(bf16[512,256]{1,0:T(8,128)(2,1)} %refs_0_.3), channel_id=1, source_target_pairs={{0,4},{1,5},{2,6},{3,7},{4,0},{5,1},{6,2},{7,3},{8,12},{9,13},{10,... | collective-permute-start | bytes 786440 | tf_op jit(solution)/shard_map/ppermute | solution.py:358
  11.1 2.1 %prep.1 = bf16[32,2,16,256]{3,2,1,0:T(8,128)(2,1)} custom-call(bf16[512,256]{1,0:T(8,128)(2,1)} %refs_3_.3, bf16[512,256]{1,0:T(8,128)(2,1)} %refs_4_.3, f32[512,256]{1,0:T(8,128)} %refs_2_.2), custom_call_target="tpu_custom_call" | custom-call | flops 3000000000 | bytes 9000000 | tf_op jit(solution)/shard_map/prep/pallas_call | solution.py:182
  13.2 0.0 collective-permute-done.2.refs_3_
  13.2 0.0 collective-permute-done.1.refs_2_
  13.2 0.0 copy-start.12
  13.3 7.8 %collective-permute-done.refs_1_ = bf16[512,256]{1,0:T(8,128)(2,1)S(1)} collective-permute-done((bf16[512,256]{1,0:T(8,128)(2,1)}, bf16[512,256]{1,0:T(8,128)(2,1)S(1)}, u32[]{:S(2)}, u32[]{:S(2)}) %collective-permute-start) | collective-permute-done | bytes 262176 | tf_op jit(solution)/shard_map/ppermute | solution.py:357
  21.1 0.0 collective-permute-done.3.refs_4_
  21.1 7.9 %all-to-all-start = ((bf16[32,2,16,256]{3,2,1,0:T(8,128)(2,1)}), bf16[32,2,16,256]{3,2,1,0:T(8,128)(2,1)S(1)}, u32[]{:S(2)}, u32[]{:S(2)}) async-start(bf16[32,2,16,256]{3,2,1,0:T(8,128)(2,1)} %prep.1), calls=%async_computation | async-start | bytes 1048576 | tf_op jit(solution)/shard_map/all_to_all | solution.py:348
  29.1 6.5 %copy.15 = bf16[4096,512]{0,1:T(8,128)(2,1)} copy(bf16[4096,512]{1,0:T(8,128)(2,1)} %param.18) | data formatting | bytes 8388608 | tf_op args[6]
  35.5 0.7 stack.48.place_ref
  36.2 1.6 %collective-permute-start.6 = (bf16[512,256]{1,0:T(8,128)(2,1)S(1)}, bf16[512,256]{1,0:T(8,128)(2,1)S(1)}, u32[]{:S(2)}, u32[]{:S(2)}) collective-permute-start(bf16[512,256]{1,0:T(8,128)(2,1)S(1)} %collective-permute-done.refs_1_), channel_id=1, source_target_pairs={{0,4},{1,5},{2,6},{3,7},{4,0},{5,1},{6,2},{7,3},{8,12},{9,13},{10,... | collective-permute-start | bytes 786440 | tf_op jit(solution)/shard_map/ppermute | solution.py:364
  37.8 1.0 collective-permute-start.5
  38.9 0.6 collective-permute-start.4
  39.4 2.7 %all-to-all-done.refs_0_ = bf16[32,2,16,256]{3,2,1,0:T(8,128)(2,1)S(1)} async-done(((bf16[32,2,16,256]{3,2,1,0:T(8,128)(2,1)}), bf16[32,2,16,256]{3,2,1,0:T(8,128)(2,1)S(1)}, u32[]{:S(2)}, u32[]{:S(2)}) %all-to-all-start) | async-done | bytes 524320 | tf_op jit(solution)/shard_map/all_to_all | solution.py:348
  42.1 0.8 copy-done.1
  42.9 5.8 %conv.1 = (bf16[32,16,256]{2,1,0:T(8,128)(2,1)}, f32[1152,256]{1,0:T(8,128)}, f32[1152,256]{1,0:T(8,128)}) custom-call(bf16[32,2,16,256]{3,2,1,0:T(8,128)(2,1)} %copy-done.1, bf16[144,128]{1,0:T(8,128)(2,1)} %constant.116.clone.refs_1_.refs_3_, bf16[2,256,256]{2,1,0:T(8,128)(2,1)} %constant.117.clone.refs_2_.refs_4_, ...), custom_call_target="tpu_custom_call" | custom-call | flops 30000001024 | bytes 90000000 | tf_op jit(solution)/shard_map/conv/pallas_call | solution.py:182
  48.7 7.4 %all-to-all-start.1 = ((bf16[32,16,256]{2,1,0:T(8,128)(2,1)}), bf16[32,16,256]{2,1,0:T(8,128)(2,1)S(1)}, u32[]{:S(2)}, u32[]{:S(2)}) async-start(bf16[32,16,256]{2,1,0:T(8,128)(2,1)} %get-tuple-element.39), calls=%async_computation.1 | async-start | bytes 524288 | tf_op jit(solution)/shard_map/all_to_all | solution.py:348
  56.1 0.0 collective-permute-done.6.refs_7_
  56.1 0.0 collective-permute-done.5.refs_6_
  56.1 0.0 collective-permute-done.4.refs_5_
  56.1 0.0 copy-start.18
  56.2 0.7 copy-done.16
  56.8 0.1 copy-done.17
  56.9 0.1 copy-done.18
  57.0 6.1 %inner.1 = (bf16[512,256]{1,0:T(8,128)(2,1)}, bf16[512,256]{1,0:T(8,128)(2,1)}, bf16[16,128,256]{2,1,0:T(8,128)(2,1)}, bf16[16,128,256]{2,1,0:T(8,128)(2,1)}) custom-call(s32[9]{0:T(128)} %stack.48.place_ref, bf16[512,4096]{1,0:T(8,128)(2,1)} %bitcast.16, bf16[512,256]{1,0:T(8,128)(2,1)} %query_hbm.1, bf16[512,256]{1,0:T(8,128)(2,1)} %refs_0_.3, ...), custom_call_target="tpu_custom_call" | custom-call | flops 30000001024 | bytes 90000000 | tf_op jit(solution)/shard_map/inner/pallas_call | solution.py:254
  63.0 1.2 all-to-all-done.1
  64.3 0.8 collective-permute-start.7
  65.1 0.1 multiply_convert_fusion.refs_3_
  65.2 0.0 copy-start.4
  65.2 0.1 collective-permute-start.8
  65.3 6.4 %all-to-all-start.2 = ((bf16[32,16,256]{2,1,0:T(8,128)(2,1)}), bf16[32,16,256]{2,1,0:T(8,128)(2,1)S(1)}, u32[]{:S(2)}, u32[]{:S(2)}) async-start(bf16[32,16,256]{2,1,0:T(8,128)(2,1)} %bitcast.18), calls=%async_computation.2 | async-start | bytes 524288 | tf_op jit(solution)/shard_map/all_to_all | solution.py:348
  71.8 0.7 pad_add_fusion.refs_0_
  72.4 0.0 collective-permute-done.7.refs_2_
  72.5 0.7 copy-done.15
  73.1 0.4 copy-done.7
  73.5 4.5 %weight.1 = (f32[4,128,512]{2,1,0:T(8,128)}, bf16[4,128,512]{2,1,0:T(8,128)(2,1)}, bf16[4,128,512]{2,1,0:T(8,128)(2,1)}, bf16[4,128,512]{2,1,0:T(8,128)(2,1)}) custom-call(s32[2]{0:T(128)} %pad_add_fusion.refs_0_, bf16[16,128,256]{2,1,0:T(8,128)(2,1)} %get-tuple-element.48.refs_1_, bf16[16,128,256]{2,1,0:T(8,128)(2,1)} %copy-done.7, ...), custom_call_target="tpu_custom_call" | custom-call | flops 3000000000 | bytes 9000000 | tf_op jit(solution)/shard_map/weight/pallas_call | solution.py:182
  78.0 0.3 collective-permute-start.9
  78.4 2.1 %collective-permute-start.10 = (bf16[4,128,512]{2,1,0:T(8,128)(2,1)}, bf16[4,128,512]{2,1,0:T(8,128)(2,1)S(1)}, u32[]{:S(2)}, u32[]{:S(2)}) collective-permute-start(bf16[4,128,512]{2,1,0:T(8,128)(2,1)} %get-tuple-element.57), channel_id=1, source_target_pairs={{0,32},{8,40},{16,48},{24,56},{32,0},{40,8},{48,16},{56,24},{64,96... | collective-permute-start | bytes 1572872 | tf_op jit(solution)/shard_map/ppermute | solution.py:406
  80.4 0.0 all-to-all-done.2.refs_0_
  80.5 0.7 copy-done.6
  81.2 6.0 %grad.1 = bf16[32,2,16,256]{3,2,1,0:T(8,128)(2,1)} custom-call(bf16[32,16,256]{2,1,0:T(8,128)(2,1)} %copy-done.6, f32[1152,256]{1,0:T(8,128)} %get-tuple-element.53.refs_1_, f32[1152,256]{1,0:T(8,128)} %get-tuple-element.54.refs_2_, bf16[144,128]{1,0:T(8,128)(2,1)} %constant.116.clone.refs_1_.refs_3_, bf16[2,256,256]{2,1,0:T(8,128)(2,1)} %constant.117.clone.refs_2_.refs_4_, ...), custom_call_target="tpu_custom_call" | custom-call | flops 5000000000 | bytes 15000000 | tf_op jit(solution)/shard_map/grad/pallas_call | solution.py:182
  87.2 8.6 %all-to-all-start.3 = ((bf16[32,2,16,256]{3,2,1,0:T(8,128)(2,1)}), bf16[32,2,16,256]{3,2,1,0:T(8,128)(2,1)S(1)}, u32[]{:S(2)}, u32[]{:S(2)}) async-start(bf16[32,2,16,256]{3,2,1,0:T(8,128)(2,1)} %grad.1), calls=%async_computation.3 | async-start | bytes 1048576 | tf_op jit(solution)/shard_map/all_to_all | solution.py:348
  95.8 0.0 copy-start.8
  95.8 0.0 collective-permute-done.10.refs_3_
  95.9 13.8 %collective-permute-done.11.refs_4_ = bf16[4,128,512]{2,1,0:T(8,128)(2,1)S(1)} collective-permute-done((bf16[4,128,512]{2,1,0:T(8,128)(2,1)}, bf16[4,128,512]{2,1,0:T(8,128)(2,1)S(1)}, u32[]{:S(2)}, u32[]{:S(2)}) %collective-permute-start.11) | collective-permute-done | bytes 524320 | tf_op jit(solution)/shard_map/ppermute | solution.py:406
  109.6 0.8 copy-done.10
  110.4 3.3 %fold.1 = (f32[128,512]{1,0:T(8,128)}, bf16[128,512]{1,0:T(8,128)(2,1)}, bf16[128,512]{1,0:T(8,128)(2,1)}, bf16[128,512]{1,0:T(8,128)(2,1)}) custom-call(s32[2]{0:T(128)} %pad_add_fusion.refs_0_, f32[4,128,512]{2,1,0:T(8,128)} %get-tuple-element.55.refs_1_, bf16[4,128,512]{2,1,0:T(8,128)(2,1)} %copy-done.8, bf16[4,128,512]{2,1,0:T(8,128)(2,1)} %copy-done.9, ...), custom_call_target="tpu_custom_call" | custom-call | flops 30000001024 | bytes 90000000 | tf_op jit(solution)/shard_map/fold/pallas_call | solution.py:182
  113.7 0.0 all-to-all-done.3.refs_0_
  113.7 0.0 copy-start.2
  113.7 0.8 copy-done.2
  114.5 2.8 %post.1 = (bf16[3,512,256]{2,1,0:T(8,128)(2,1)}, bf16[512,128]{1,0:T(8,128)(2,1)}, f32[512,256]{1,0:T(8,128)}) custom-call(bf16[32,2,16,256]{3,2,1,0:T(8,128)(2,1)} %copy-done.2, bf16[512,256]{1,0:T(8,128)(2,1)} %get-tuple-element.62.refs_1_, bf16[512,256]{1,0:T(8,128)(2,1)} %bitcast.17, bf16[512,256]{1,0:T(8,128)(2,1)} %refs_3_.3, bf16[512,256]{1,0:T(8,128)(2,1)} %refs_4_.3), custom_call_target="tpu_custom_call" | custom-call | flops 3000000000 | bytes 9000000 | tf_op jit(solution)/shard_map/post/pallas_call | solution.py:182
  117.3 2.6 %collective-permute-start.12 = (bf16[512,128]{1,0:T(8,128)(2,1)}, bf16[512,128]{1,0:T(8,128)(2,1)S(1)}, u32[]{:S(2)}, u32[]{:S(2)}) collective-permute-start(bf16[512,128]{1,0:T(8,128)(2,1)} %get-tuple-element.64), channel_id=1, source_target_pairs={{8,0},{16,8},{24,16},{32,24},{40,32},{48,40},{56,48},{64,56},{72,6... | collective-permute-start | bytes 393224 | tf_op jit(solution)/shard_map/ppermute | solution.py:447
  119.9 1.3 collective-permute-start.13
  121.2 1.1 collective-permute-start.14
  122.2 1.4 collective-permute-start.15
  123.6 7.9 %collective-permute-done.12.refs_1_ = bf16[512,128]{1,0:T(8,128)(2,1)S(1)} collective-permute-done((bf16[512,128]{1,0:T(8,128)(2,1)}, bf16[512,128]{1,0:T(8,128)(2,1)S(1)}, u32[]{:S(2)}, u32[]{:S(2)}) %collective-permute-start.12) | collective-permute-done | bytes 131104 | tf_op jit(solution)/shard_map/ppermute | solution.py:447
  131.5 0.6 copy-done.22
  132.2 6.7 %feature.1 = bf16[3,512,256]{2,1,0:T(8,128)(2,1)} custom-call(bf16[3,512,256]{2,1,0:T(8,128)(2,1)} %get-tuple-element.63.refs_0_, bf16[512,128]{1,0:T(8,128)(2,1)} %copy-done.22, f32[3,7,512]{2,1,0:T(8,128)} %bitcast.19), custom_call_target="tpu_custom_call" | custom-call | flops 3000000000 | bytes 9000000 | tf_op jit(solution)/shard_map/feature/pallas_call | solution.py:182
  138.9 0.0 collective-permute-done.14
  138.9 0.0 collective-permute-done.15
  138.9 0.8 add_add_fusion
  (35 shorter events, 0.1 us)
Async XLA Ops:
  0.6 12.6 %collective-permute-start.2 = (bf16[512,256]{1,0:T(8,128)(2,1)}, bf16[512,256]{1,0:T(8,128)(2,1)S(1)}, u32[]{:S(2)}, u32[]{:S(2)}) collective-permute-start(bf16[512,256]{1,0:T(8,128)(2,1)} %refs_0_.3), channel_id=1, source_target_pairs={{0,6},{1,7},{2,0},{3,1},{4,2},{5,3},{6,4},{7,5},{8,14},{9,15},{10,... | collective-permute-start | bytes 786440 | tf_op jit(solution)/shard_map/ppermute | solution.py:358
  3.4 9.8 %collective-permute-start.1 = (bf16[512,256]{1,0:T(8,128)(2,1)}, bf16[512,256]{1,0:T(8,128)(2,1)S(1)}, u32[]{:S(2)}, u32[]{:S(2)}) collective-permute-start(bf16[512,256]{1,0:T(8,128)(2,1)} %refs_0_.3), channel_id=1, source_target_pairs={{0,2},{1,3},{2,4},{3,5},{4,6},{5,7},{6,0},{7,1},{8,10},{9,11},{10,... | collective-permute-start | bytes 786440 | tf_op jit(solution)/shard_map/ppermute | solution.py:358
  3.4 17.6 %collective-permute-start = (bf16[512,256]{1,0:T(8,128)(2,1)}, bf16[512,256]{1,0:T(8,128)(2,1)S(1)}, u32[]{:S(2)}, u32[]{:S(2)}) collective-permute-start(bf16[512,256]{1,0:T(8,128)(2,1)} %refs_0_.3), channel_id=1, source_target_pairs={{0,1},{1,0},{2,3},{3,2},{4,5},{5,4},{6,7},{7,6},{8,9},{9,8},{10,11... | collective-permute-start | bytes 786440 | tf_op jit(solution)/shard_map/ppermute | solution.py:357
  9.5 11.6 %collective-permute-start.3 = (bf16[512,256]{1,0:T(8,128)(2,1)}, bf16[512,256]{1,0:T(8,128)(2,1)S(1)}, u32[]{:S(2)}, u32[]{:S(2)}) collective-permute-start(bf16[512,256]{1,0:T(8,128)(2,1)} %refs_0_.3), channel_id=1, source_target_pairs={{0,4},{1,5},{2,6},{3,7},{4,0},{5,1},{6,2},{7,3},{8,12},{9,13},{10,... | collective-permute-start | bytes 786440 | tf_op jit(solution)/shard_map/ppermute | solution.py:358
  13.2 22.3 %copy-start.11 = (bf16[512,256]{1,0:T(8,128)(2,1)}, bf16[512,256]{1,0:T(8,128)(2,1)S(1)}, u32[]{:S(2)}) copy-start(bf16[512,256]{1,0:T(8,128)(2,1)S(1)} %collective-permute-done.2.refs_3_) | copy-start | bytes 786436
  13.2 22.3 %copy-start.12 = (bf16[512,256]{1,0:T(8,128)(2,1)}, bf16[512,256]{1,0:T(8,128)(2,1)S(1)}, u32[]{:S(2)}) copy-start(bf16[512,256]{1,0:T(8,128)(2,1)S(1)} %collective-permute-done.1.refs_2_) | copy-start | bytes 786436
  21.1 17.8 %copy-start.13 = (bf16[512,256]{1,0:T(8,128)(2,1)}, bf16[512,256]{1,0:T(8,128)(2,1)S(1)}, u32[]{:S(2)}) copy-start(bf16[512,256]{1,0:T(8,128)(2,1)S(1)} %collective-permute-done.refs_1_) | copy-start | bytes 786436
  21.1 14.5 %copy-start.14 = (bf16[512,256]{1,0:T(8,128)(2,1)}, bf16[512,256]{1,0:T(8,128)(2,1)S(1)}, u32[]{:S(2)}) copy-start(bf16[512,256]{1,0:T(8,128)(2,1)S(1)} %collective-permute-done.3.refs_4_) | copy-start | bytes 786436
  21.1 21.1 %all-to-all-start = ((bf16[32,2,16,256]{3,2,1,0:T(8,128)(2,1)}), bf16[32,2,16,256]{3,2,1,0:T(8,128)(2,1)S(1)}, u32[]{:S(2)}, u32[]{:S(2)}) async-start(bf16[32,2,16,256]{3,2,1,0:T(8,128)(2,1)} %prep.1), calls=%async_computation | async-start | bytes 1048576 | tf_op jit(solution)/shard_map/all_to_all | solution.py:348
  36.2 19.9 %collective-permute-start.6 = (bf16[512,256]{1,0:T(8,128)(2,1)S(1)}, bf16[512,256]{1,0:T(8,128)(2,1)S(1)}, u32[]{:S(2)}, u32[]{:S(2)}) collective-permute-start(bf16[512,256]{1,0:T(8,128)(2,1)S(1)} %collective-permute-done.refs_1_), channel_id=1, source_target_pairs={{0,4},{1,5},{2,6},{3,7},{4,0},{5,1},{6,2},{7,3},{8,12},{9,13},{10,... | collective-permute-start | bytes 786440 | tf_op jit(solution)/shard_map/ppermute | solution.py:364
  37.8 18.3 %collective-permute-start.5 = (bf16[512,256]{1,0:T(8,128)(2,1)S(1)}, bf16[512,256]{1,0:T(8,128)(2,1)S(1)}, u32[]{:S(2)}, u32[]{:S(2)}) collective-permute-start(bf16[512,256]{1,0:T(8,128)(2,1)S(1)} %collective-permute-done.refs_1_), channel_id=1, source_target_pairs={{0,6},{1,7},{2,0},{3,1},{4,2},{5,3},{6,4},{7,5},{8,14},{9,15},{10,... | collective-permute-start | bytes 786440 | tf_op jit(solution)/shard_map/ppermute | solution.py:364
  38.9 17.3 %collective-permute-start.4 = (bf16[512,256]{1,0:T(8,128)(2,1)S(1)}, bf16[512,256]{1,0:T(8,128)(2,1)S(1)}, u32[]{:S(2)}, u32[]{:S(2)}) collective-permute-start(bf16[512,256]{1,0:T(8,128)(2,1)S(1)} %collective-permute-done.refs_1_), channel_id=1, source_target_pairs={{0,2},{1,3},{2,4},{3,5},{4,6},{5,7},{6,0},{7,1},{8,10},{9,11},{10,... | collective-permute-start | bytes 786440 | tf_op jit(solution)/shard_map/ppermute | solution.py:364
  42.1 0.8 copy-start.1
  48.7 15.6 %all-to-all-start.1 = ((bf16[32,16,256]{2,1,0:T(8,128)(2,1)}), bf16[32,16,256]{2,1,0:T(8,128)(2,1)S(1)}, u32[]{:S(2)}, u32[]{:S(2)}) async-start(bf16[32,16,256]{2,1,0:T(8,128)(2,1)} %get-tuple-element.39), calls=%async_computation.1 | async-start | bytes 524288 | tf_op jit(solution)/shard_map/all_to_all | solution.py:348
  56.1 0.7 copy-start.16
  56.1 0.8 copy-start.17
  56.1 0.8 copy-start.18
  57.0 8.1 %copy-start.3 = (bf16[512,256]{1,0:T(8,128)(2,1)S(1)}, bf16[512,256]{1,0:T(8,128)(2,1)}, u32[]{:S(2)}) copy-start(bf16[512,256]{1,0:T(8,128)(2,1)} %query_hbm.1) | copy-start | bytes 786436
  64.3 13.7 %copy-start = (bf16[32,16,256]{2,1,0:T(8,128)(2,1)}, bf16[32,16,256]{2,1,0:T(8,128)(2,1)S(1)}, u32[]{:S(2)}) copy-start(bf16[32,16,256]{2,1,0:T(8,128)(2,1)S(1)} %all-to-all-done.1) | copy-start | bytes 786436
  64.3 8.2 %collective-permute-start.7 = (bf16[16,128,256]{2,1,0:T(8,128)(2,1)}, bf16[16,128,256]{2,1,0:T(8,128)(2,1)S(1)}, u32[]{:S(2)}, u32[]{:S(2)}) collective-permute-start(bf16[16,128,256]{2,1,0:T(8,128)(2,1)} %get-tuple-element.49), channel_id=1, source_target_pairs={{0,8},{8,0},{16,24},{24,16},{32,40},{40,32},{48,56},{56,48},{64,72... | collective-permute-start | bytes 3145736 | tf_op jit(solution)/shard_map/ppermute | solution.py:389
  65.2 7.3 %copy-start.4 = (bf16[512,256]{1,0:T(8,128)(2,1)}, bf16[512,256]{1,0:T(8,128)(2,1)S(1)}, u32[]{:S(2)}) copy-start(bf16[512,256]{1,0:T(8,128)(2,1)S(1)} %multiply_convert_fusion.refs_3_) | copy-start | bytes 786436
  65.2 7.3 %collective-permute-start.8 = (bf16[512,256]{1,0:T(8,128)(2,1)S(1)}, bf16[512,256]{1,0:T(8,128)(2,1)S(1)}, u32[]{:S(2)}, u32[]{:S(2)}) collective-permute-start(bf16[512,256]{1,0:T(8,128)(2,1)S(1)} %multiply_convert_fusion.refs_3_), channel_id=1, source_target_pairs={{0,8},{8,0},{16,24},{24,16},{32,40},{40,32},{48,56},{56,48},{64,72... | collective-permute-start | bytes 786440 | tf_op jit(solution)/shard_map/ppermute | solution.py:391
  65.3 15.2 %all-to-all-start.2 = ((bf16[32,16,256]{2,1,0:T(8,128)(2,1)}), bf16[32,16,256]{2,1,0:T(8,128)(2,1)S(1)}, u32[]{:S(2)}, u32[]{:S(2)}) async-start(bf16[32,16,256]{2,1,0:T(8,128)(2,1)} %bitcast.18), calls=%async_computation.2 | async-start | bytes 524288 | tf_op jit(solution)/shard_map/all_to_all | solution.py:348
  72.4 0.7 copy-start.15
  72.5 1.1 copy-start.7
  78.0 17.8 %collective-permute-start.9 = (bf16[4,128,512]{2,1,0:T(8,128)(2,1)}, bf16[4,128,512]{2,1,0:T(8,128)(2,1)S(1)}, u32[]{:S(2)}, u32[]{:S(2)}) collective-permute-start(bf16[4,128,512]{2,1,0:T(8,128)(2,1)} %get-tuple-element.56), channel_id=1, source_target_pairs={{0,16},{8,24},{16,32},{24,40},{32,48},{40,56},{48,0},{56,8},{64,80... | collective-permute-start | bytes 1572872 | tf_op jit(solution)/shard_map/ppermute | solution.py:406
  78.4 17.5 %collective-permute-start.10 = (bf16[4,128,512]{2,1,0:T(8,128)(2,1)}, bf16[4,128,512]{2,1,0:T(8,128)(2,1)S(1)}, u32[]{:S(2)}, u32[]{:S(2)}) collective-permute-start(bf16[4,128,512]{2,1,0:T(8,128)(2,1)} %get-tuple-element.57), channel_id=1, source_target_pairs={{0,32},{8,40},{16,48},{24,56},{32,0},{40,8},{48,16},{56,24},{64,96... | collective-permute-start | bytes 1572872 | tf_op jit(solution)/shard_map/ppermute | solution.py:406
  80.4 29.2 %collective-permute-start.11 = (bf16[4,128,512]{2,1,0:T(8,128)(2,1)}, bf16[4,128,512]{2,1,0:T(8,128)(2,1)S(1)}, u32[]{:S(2)}, u32[]{:S(2)}) collective-permute-start(bf16[4,128,512]{2,1,0:T(8,128)(2,1)} %get-tuple-element.58), channel_id=1, source_target_pairs={{0,48},{8,56},{16,0},{24,8},{32,16},{40,24},{48,32},{56,40},{64,11... | collective-permute-start | bytes 1572872 | tf_op jit(solution)/shard_map/ppermute | solution.py:406
  80.4 0.7 copy-start.6
  87.2 26.5 %all-to-all-start.3 = ((bf16[32,2,16,256]{3,2,1,0:T(8,128)(2,1)}), bf16[32,2,16,256]{3,2,1,0:T(8,128)(2,1)S(1)}, u32[]{:S(2)}, u32[]{:S(2)}) async-start(bf16[32,2,16,256]{3,2,1,0:T(8,128)(2,1)} %grad.1), calls=%async_computation.3 | async-start | bytes 1048576 | tf_op jit(solution)/shard_map/all_to_all | solution.py:348
  95.8 13.8 %copy-start.8 = (bf16[4,128,512]{2,1,0:T(8,128)(2,1)}, bf16[4,128,512]{2,1,0:T(8,128)(2,1)S(1)}, u32[]{:S(2)}) copy-start(bf16[4,128,512]{2,1,0:T(8,128)(2,1)S(1)} %collective-permute-done.9.refs_2_) | copy-start | bytes 1572868
  95.9 13.8 %copy-start.9 = (bf16[4,128,512]{2,1,0:T(8,128)(2,1)}, bf16[4,128,512]{2,1,0:T(8,128)(2,1)S(1)}, u32[]{:S(2)}) copy-start(bf16[4,128,512]{2,1,0:T(8,128)(2,1)S(1)} %collective-permute-done.10.refs_3_) | copy-start | bytes 1572868
  109.6 0.8 copy-start.10
  113.7 0.8 copy-start.2
  114.5 5.3 %copy-start.21 = (bf16[128,512]{1,0:T(8,128)(2,1)S(1)}, bf16[128,512]{1,0:T(8,128)(2,1)}, u32[]{:S(2)}) copy-start(bf16[128,512]{1,0:T(8,128)(2,1)} %get-tuple-element.68) | copy-start | bytes 393220
  114.5 6.6 %copy-start.20 = (bf16[128,512]{1,0:T(8,128)(2,1)S(1)}, bf16[128,512]{1,0:T(8,128)(2,1)}, u32[]{:S(2)}) copy-start(bf16[128,512]{1,0:T(8,128)(2,1)} %get-tuple-element.69) | copy-start | bytes 393220
  114.5 7.7 %copy-start.19 = (bf16[128,512]{1,0:T(8,128)(2,1)S(1)}, bf16[128,512]{1,0:T(8,128)(2,1)}, u32[]{:S(2)}) copy-start(bf16[128,512]{1,0:T(8,128)(2,1)} %get-tuple-element.70) | copy-start | bytes 393220
  117.3 14.2 %collective-permute-start.12 = (bf16[512,128]{1,0:T(8,128)(2,1)}, bf16[512,128]{1,0:T(8,128)(2,1)S(1)}, u32[]{:S(2)}, u32[]{:S(2)}) collective-permute-start(bf16[512,128]{1,0:T(8,128)(2,1)} %get-tuple-element.64), channel_id=1, source_target_pairs={{8,0},{16,8},{24,16},{32,24},{40,32},{48,40},{56,48},{64,56},{72,6... | collective-permute-start | bytes 393224 | tf_op jit(solution)/shard_map/ppermute | solution.py:447
  119.9 19.0 %collective-permute-start.13 = (bf16[128,512]{1,0:T(8,128)(2,1)S(1)}, bf16[128,512]{1,0:T(8,128)(2,1)S(1)}, u32[]{:S(2)}, u32[]{:S(2)}) collective-permute-start(bf16[128,512]{1,0:T(8,128)(2,1)S(1)} %copy-done.21), channel_id=1, source_target_pairs={{0,64},{8,72},{16,80},{24,88},{32,96},{40,104},{48,112},{56,120},{... | collective-permute-start | bytes 393224 | tf_op jit(solution)/shard_map/ppermute | solution.py:434
  121.2 17.7 %collective-permute-start.14 = (bf16[128,512]{1,0:T(8,128)(2,1)S(1)}, bf16[128,512]{1,0:T(8,128)(2,1)S(1)}, u32[]{:S(2)}, u32[]{:S(2)}) collective-permute-start(bf16[128,512]{1,0:T(8,128)(2,1)S(1)} %copy-done.20), channel_id=1, source_target_pairs={{0,128},{8,136},{16,144},{24,152},{32,160},{40,168},{48,176},{56,1... | collective-permute-start | bytes 393224 | tf_op jit(solution)/shard_map/ppermute | solution.py:434
  122.2 16.6 %collective-permute-start.15 = (bf16[128,512]{1,0:T(8,128)(2,1)S(1)}, bf16[128,512]{1,0:T(8,128)(2,1)S(1)}, u32[]{:S(2)}, u32[]{:S(2)}) collective-permute-start(bf16[128,512]{1,0:T(8,128)(2,1)S(1)} %copy-done.19), channel_id=1, source_target_pairs={{0,192},{8,200},{16,208},{24,216},{32,224},{40,232},{48,240},{56,2... | collective-permute-start | bytes 393224 | tf_op jit(solution)/shard_map/ppermute | solution.py:434
  131.5 0.6 copy-start.22
  132.2 6.7 %copy-start.5 = (f32[128,512]{1,0:T(8,128)S(1)}, f32[128,512]{1,0:T(8,128)}, u32[]{:S(2)}) copy-start(f32[128,512]{1,0:T(8,128)} %get-tuple-element.67) | copy-start | bytes 786436

commit v4 on v3

--- a/solution.py
+++ b/solution.py
@@ -132,9 +132,13 @@
     out_ref[:, 1] = filter_ref[...].astype(BF).reshape(CTX, CH, LOC)
 
 
-def conv_kernel(in_ref, first, forward, inverse, twiddle, last, out_ref, kv_spec, fil_spec, work):
+def conv_kernel(
+    in_ref, first, forward, inverse, twiddle, last, out_ref, kv_spec, fil_spec, work, early
+):
     forward_spectrum(in_ref[:, 0], first, forward, twiddle, work, kv_spec)
+    early[0]()
     forward_spectrum(in_ref[:, 1], first, forward, twiddle, work, fil_spec)
+    early[1]()
     times(fil_spec, kv_spec, 1, work)
     out_ref[...] = inverse_signal(work, inverse, twiddle, last).astype(BF)
 
@@ -149,7 +153,7 @@
     out_ref[:, 1] = inverse_signal(work, inverse, twiddle, last).astype(BF)
 
 
-def staged(kernel, scalars, ins, outs):
+def staged(kernel, scalars, ins, outs, flushed):
     def body(*refs):
         at = scalars + ins
         far_in, far_out = refs[scalars:at], refs[at : at + outs]
@@ -163,11 +167,13 @@
             load.start()
         for load in loads:
             load.wait()
-        kernel(*refs[:scalars], *near_in, *near_out, *refs[at + ins + outs + 1 :])
         stores = [
             pltpu.make_async_copy(near_out[i], far_out[i], sems.at[ins + i]) for i in range(outs)
         ]
-        for store in stores:
+        early = [stores[i].start for i in range(outs - flushed, outs)]
+        extra = (early,) if flushed else ()
+        kernel(*refs[:scalars], *near_in, *near_out, *refs[at + ins + outs + 1 :], *extra)
+        for store in stores[: outs - flushed]:
             store.start()
         for store in stores:
             store.wait()
@@ -175,12 +181,12 @@
     return body
 
 
-def call(kernel, outs, *args, scalars=0, scratch=(), name=None, us=3):
+def call(kernel, outs, *args, scalars=0, scratch=(), name=None, us=3, flushed=0):
     arrays = args[scalars:]
     hbm = pl.BlockSpec(memory_space=pltpu.HBM)
     specs = [pl.BlockSpec(memory_space=pltpu.SMEM)] * scalars + [hbm] * len(arrays)
     return pl.pallas_call(
-        staged(kernel, scalars, len(arrays), len(outs)),
+        staged(kernel, scalars, len(arrays), len(outs), flushed),
         out_shape=[jax.ShapeDtypeStruct(shape, dtype) for shape, dtype in outs],
         in_specs=specs,
         out_specs=[hbm] * len(outs),
@@ -378,6 +384,7 @@
         *tables,
         scratch=[pltpu.VMEM(*spec_shape)],
         name="conv",
+        flushed=2,
         us=30,
     )
     conv_cols, place = lax.optimization_barrier((conv_cols, place))

time: 140 us -> 140 us (level)
  transfers between devices with their start and end apart: 20 -> 20, of which waited for: 5 -> 5; matrix products, arithmetic and copies ran while one was open for 6% -> 6% of each run, Pallas kernels for 25% -> 24%
where the time goes in v4:
time: 140 us; the launch traced here: 139 us
  starting transfers between devices  53.7 us (38%)
  Pallas kernels  36.3 us (26%)
  waiting for transfers between devices  33.5 us (24%)
  local copies, waits for them, and re-layouts  12.8 us (9%)
  other arithmetic  1.51 us (1%)
    all_to_all x4, starting transfers between devices, exchange(): return lax.all_to_all(value, 'ctx', split_axis=0, concat_axis=0, tiled=True)  30.3 us
    pallas_call x7, Pallas kernels, call(): pl.pallas_call(staged(kernel, scalars, len(arrays), len(outs), flushed),...  30.3 us
    ppermute x3, waiting for transfers between devices, local(): lax.ppermute(to_x[step - 1], 'ctx', ctx_shift(0, step, 0))  13.8 us
    unnamed x47, local copies, waits for them, and re-layouts  12.1 us
    ppermute x1, waiting for transfers between devices, local(): lax.ppermute(halo, 'ctx', [(source, source - 1) for source in range(1, CT...  7.91 us
    ppermute x1, waiting for transfers between devices, local(): far = lax.ppermute(out_cotangent, 'tp', tp_shift(0, 1))  7.8 us
    pallas_call x1, Pallas kernels, inner_call(): pl.pallas_call(inner_kernel, out_shape=[jax.ShapeDtypeStruct(shape, BF) f...  6.06 us
    ppermute x1, starting transfers between devices, local(): far = lax.ppermute(out_cotangent, 'tp', tp_shift(0, 1))  6.01 us
  transfers between devices with their start and end apart: 20, of which 5 were waited for; matrix products, arithmetic and copies ran while one was open for 6% of the time, Pallas kernels for 24%

profile of v4, /device:TPU:39, one launch (start us, length us, event | category | flops | bytes accessed | tf_op | source)
XLA Modules:
  0.0 138.8 jit_solution(1145194674910803086)
XLA Ops:
  0.6 2.8 %collective-permute-start.2 = (bf16[512,256]{1,0:T(8,128)(2,1)}, bf16[512,256]{1,0:T(8,128)(2,1)S(1)}, u32[]{:S(2)}, u32[]{:S(2)}) collective-permute-start(bf16[512,256]{1,0:T(8,128)(2,1)} %refs_0_.3), channel_id=1, source_target_pairs={{0,6},{1,7},{2,0},{3,1},{4,2},{5,3},{6,4},{7,5},{8,14},{9,15},{10,... | collective-permute-start | bytes 786440 | tf_op jit(solution)/shard_map/ppermute | solution.py:364
  3.4 0.0 collective-permute-start.1
  3.4 6.0 %collective-permute-start = (bf16[512,256]{1,0:T(8,128)(2,1)}, bf16[512,256]{1,0:T(8,128)(2,1)S(1)}, u32[]{:S(2)}, u32[]{:S(2)}) collective-permute-start(bf16[512,256]{1,0:T(8,128)(2,1)} %refs_0_.3), channel_id=1, source_target_pairs={{0,1},{1,0},{2,3},{3,2},{4,5},{5,4},{6,7},{7,6},{8,9},{9,8},{10,11... | collective-permute-start | bytes 786440 | tf_op jit(solution)/shard_map/ppermute | solution.py:363
  9.5 1.6 %collective-permute-start.3 = (bf16[512,256]{1,0:T(8,128)(2,1)}, bf16[512,256]{1,0:T(8,128)(2,1)S(1)}, u32[]{:S(2)}, u32[]{:S(2)}) collective-permute-start(bf16[512,256]{1,0:T(8,128)(2,1)} %refs_0_.3), channel_id=1, source_target_pairs={{0,4},{1,5},{2,6},{3,7},{4,0},{5,1},{6,2},{7,3},{8,12},{9,13},{10,... | collective-permute-start | bytes 786440 | tf_op jit(solution)/shard_map/ppermute | solution.py:364
  11.1 2.1 %prep.1 = bf16[32,2,16,256]{3,2,1,0:T(8,128)(2,1)} custom-call(bf16[512,256]{1,0:T(8,128)(2,1)} %refs_3_.3, bf16[512,256]{1,0:T(8,128)(2,1)} %refs_4_.3, f32[512,256]{1,0:T(8,128)} %refs_2_.2), custom_call_target="tpu_custom_call" | custom-call | flops 3000000000 | bytes 9000000 | tf_op jit(solution)/shard_map/prep/pallas_call | solution.py:188
  13.2 0.0 collective-permute-done.2.refs_3_
  13.2 0.0 collective-permute-done.1.refs_2_
  13.2 0.0 copy-start.12
  13.3 7.8 %collective-permute-done.refs_1_ = bf16[512,256]{1,0:T(8,128)(2,1)S(1)} collective-permute-done((bf16[512,256]{1,0:T(8,128)(2,1)}, bf16[512,256]{1,0:T(8,128)(2,1)S(1)}, u32[]{:S(2)}, u32[]{:S(2)}) %collective-permute-start) | collective-permute-done | bytes 262176 | tf_op jit(solution)/shard_map/ppermute | solution.py:363
  21.1 0.0 collective-permute-done.3.refs_4_
  21.1 7.9 %all-to-all-start = ((bf16[32,2,16,256]{3,2,1,0:T(8,128)(2,1)}), bf16[32,2,16,256]{3,2,1,0:T(8,128)(2,1)S(1)}, u32[]{:S(2)}, u32[]{:S(2)}) async-start(bf16[32,2,16,256]{3,2,1,0:T(8,128)(2,1)} %prep.1), calls=%async_computation | async-start | bytes 1048576 | tf_op jit(solution)/shard_map/all_to_all | solution.py:354
  29.1 6.5 %copy.15 = bf16[4096,512]{0,1:T(8,128)(2,1)} copy(bf16[4096,512]{1,0:T(8,128)(2,1)} %param.18) | data formatting | bytes 8388608 | tf_op args[6]
  35.5 0.7 stack.48.place_ref
  36.2 1.6 %collective-permute-start.6 = (bf16[512,256]{1,0:T(8,128)(2,1)S(1)}, bf16[512,256]{1,0:T(8,128)(2,1)S(1)}, u32[]{:S(2)}, u32[]{:S(2)}) collective-permute-start(bf16[512,256]{1,0:T(8,128)(2,1)S(1)} %collective-permute-done.refs_1_), channel_id=1, source_target_pairs={{0,4},{1,5},{2,6},{3,7},{4,0},{5,1},{6,2},{7,3},{8,12},{9,13},{10,... | collective-permute-start | bytes 786440 | tf_op jit(solution)/shard_map/ppermute | solution.py:370
  37.8 1.0 collective-permute-start.5
  38.9 0.6 collective-permute-start.4
  39.4 2.7 %all-to-all-done.refs_0_ = bf16[32,2,16,256]{3,2,1,0:T(8,128)(2,1)S(1)} async-done(((bf16[32,2,16,256]{3,2,1,0:T(8,128)(2,1)}), bf16[32,2,16,256]{3,2,1,0:T(8,128)(2,1)S(1)}, u32[]{:S(2)}, u32[]{:S(2)}) %all-to-all-start) | async-done | bytes 524320 | tf_op jit(solution)/shard_map/all_to_all | solution.py:354
  42.1 0.8 copy-done.1
  42.9 5.0 %conv.1 = (bf16[32,16,256]{2,1,0:T(8,128)(2,1)}, f32[1152,256]{1,0:T(8,128)}, f32[1152,256]{1,0:T(8,128)}) custom-call(bf16[32,2,16,256]{3,2,1,0:T(8,128)(2,1)} %copy-done.1, bf16[144,128]{1,0:T(8,128)(2,1)} %constant.116.clone.refs_1_.refs_3_, bf16[2,256,256]{2,1,0:T(8,128)(2,1)} %constant.117.clone.refs_2_.refs_4_, ...), custom_call_target="tpu_custom_call" | custom-call | flops 30000001024 | bytes 90000000 | tf_op jit(solution)/shard_map/conv/pallas_call | solution.py:188
  47.9 7.4 %all-to-all-start.1 = ((bf16[32,16,256]{2,1,0:T(8,128)(2,1)}), bf16[32,16,256]{2,1,0:T(8,128)(2,1)S(1)}, u32[]{:S(2)}, u32[]{:S(2)}) async-start(bf16[32,16,256]{2,1,0:T(8,128)(2,1)} %get-tuple-element.39), calls=%async_computation.1 | async-start | bytes 524288 | tf_op jit(solution)/shard_map/all_to_all | solution.py:354
  55.3 0.0 collective-permute-done.6.refs_7_
  55.3 0.0 collective-permute-done.5.refs_6_
  55.3 0.0 collective-permute-done.4.refs_5_
  55.3 0.0 copy-start.18
  55.3 0.7 copy-done.16
  56.0 0.1 copy-done.17
  56.1 0.1 copy-done.18
  56.2 6.1 %inner.1 = (bf16[512,256]{1,0:T(8,128)(2,1)}, bf16[512,256]{1,0:T(8,128)(2,1)}, bf16[16,128,256]{2,1,0:T(8,128)(2,1)}, bf16[16,128,256]{2,1,0:T(8,128)(2,1)}) custom-call(s32[9]{0:T(128)} %stack.48.place_ref, bf16[512,4096]{1,0:T(8,128)(2,1)} %bitcast.16, bf16[512,256]{1,0:T(8,128)(2,1)} %query_hbm.1, bf16[512,256]{1,0:T(8,128)(2,1)} %refs_0_.3, ...), custom_call_target="tpu_custom_call" | custom-call | flops 30000001024 | bytes 90000000 | tf_op jit(solution)/shard_map/inner/pallas_call | solution.py:260
  62.2 1.2 all-to-all-done.1
  63.5 0.8 collective-permute-start.7
  64.3 0.1 multiply_convert_fusion.refs_3_
  64.4 0.0 copy-start.4
  64.4 0.1 collective-permute-start.8
  64.5 6.4 %all-to-all-start.2 = ((bf16[32,16,256]{2,1,0:T(8,128)(2,1)}), bf16[32,16,256]{2,1,0:T(8,128)(2,1)S(1)}, u32[]{:S(2)}, u32[]{:S(2)}) async-start(bf16[32,16,256]{2,1,0:T(8,128)(2,1)} %bitcast.18), calls=%async_computation.2 | async-start | bytes 524288 | tf_op jit(solution)/shard_map/all_to_all | solution.py:354
  71.0 0.7 pad_add_fusion.refs_0_
  71.6 0.0 collective-permute-done.8.refs_4_
  71.6 0.0 collective-permute-done.7.refs_2_
  71.7 0.7 copy-done.15
  72.3 0.4 copy-done.7
  72.7 4.5 %weight.1 = (f32[4,128,512]{2,1,0:T(8,128)}, bf16[4,128,512]{2,1,0:T(8,128)(2,1)}, bf16[4,128,512]{2,1,0:T(8,128)(2,1)}, bf16[4,128,512]{2,1,0:T(8,128)(2,1)}) custom-call(s32[2]{0:T(128)} %pad_add_fusion.refs_0_, bf16[16,128,256]{2,1,0:T(8,128)(2,1)} %get-tuple-element.48.refs_1_, bf16[16,128,256]{2,1,0:T(8,128)(2,1)} %copy-done.7, ...), custom_call_target="tpu_custom_call" | custom-call | flops 3000000000 | bytes 9000000 | tf_op jit(solution)/shard_map/weight/pallas_call | solution.py:188
  77.2 0.4 collective-permute-start.9
  77.5 2.1 %collective-permute-start.10 = (bf16[4,128,512]{2,1,0:T(8,128)(2,1)}, bf16[4,128,512]{2,1,0:T(8,128)(2,1)S(1)}, u32[]{:S(2)}, u32[]{:S(2)}) collective-permute-start(bf16[4,128,512]{2,1,0:T(8,128)(2,1)} %get-tuple-element.57), channel_id=1, source_target_pairs={{0,32},{8,40},{16,48},{24,56},{32,0},{40,8},{48,16},{56,24},{64,96... | collective-permute-start | bytes 1572872 | tf_op jit(solution)/shard_map/ppermute | solution.py:413
  79.6 0.7 copy-done.6
  80.3 6.0 %grad.1 = bf16[32,2,16,256]{3,2,1,0:T(8,128)(2,1)} custom-call(bf16[32,16,256]{2,1,0:T(8,128)(2,1)} %copy-done.6, f32[1152,256]{1,0:T(8,128)} %get-tuple-element.53.refs_1_, f32[1152,256]{1,0:T(8,128)} %get-tuple-element.54.refs_2_, bf16[144,128]{1,0:T(8,128)(2,1)} %constant.116.clone.refs_1_.refs_3_, bf16[2,256,256]{2,1,0:T(8,128)(2,1)} %constant.117.clone.refs_2_.refs_4_, ...), custom_call_target="tpu_custom_call" | custom-call | flops 5000000000 | bytes 15000000 | tf_op jit(solution)/shard_map/grad/pallas_call | solution.py:188
  86.4 8.6 %all-to-all-start.3 = ((bf16[32,2,16,256]{3,2,1,0:T(8,128)(2,1)}), bf16[32,2,16,256]{3,2,1,0:T(8,128)(2,1)S(1)}, u32[]{:S(2)}, u32[]{:S(2)}) async-start(bf16[32,2,16,256]{3,2,1,0:T(8,128)(2,1)} %grad.1), calls=%async_computation.3 | async-start | bytes 1048576 | tf_op jit(solution)/shard_map/all_to_all | solution.py:354
  95.0 0.0 collective-permute-done.9.refs_2_
  95.0 0.0 copy-start.8
  95.1 13.8 %collective-permute-done.11.refs_4_ = bf16[4,128,512]{2,1,0:T(8,128)(2,1)S(1)} collective-permute-done((bf16[4,128,512]{2,1,0:T(8,128)(2,1)}, bf16[4,128,512]{2,1,0:T(8,128)(2,1)S(1)}, u32[]{:S(2)}, u32[]{:S(2)}) %collective-permute-start.11) | collective-permute-done | bytes 524320 | tf_op jit(solution)/shard_map/ppermute | solution.py:413
  108.8 0.8 copy-done.10
  109.6 3.3 %fold.1 = (f32[128,512]{1,0:T(8,128)}, bf16[128,512]{1,0:T(8,128)(2,1)}, bf16[128,512]{1,0:T(8,128)(2,1)}, bf16[128,512]{1,0:T(8,128)(2,1)}) custom-call(s32[2]{0:T(128)} %pad_add_fusion.refs_0_, f32[4,128,512]{2,1,0:T(8,128)} %get-tuple-element.55.refs_1_, bf16[4,128,512]{2,1,0:T(8,128)(2,1)} %copy-done.8, bf16[4,128,512]{2,1,0:T(8,128)(2,1)} %copy-done.9, ...), custom_call_target="tpu_custom_call" | custom-call | flops 30000001024 | bytes 90000000 | tf_op jit(solution)/shard_map/fold/pallas_call | solution.py:188
  112.9 0.0 all-to-all-done.3.refs_0_
  112.9 0.0 copy-start.2
  112.9 0.8 copy-done.2
  113.7 2.8 %post.1 = (bf16[3,512,256]{2,1,0:T(8,128)(2,1)}, bf16[512,128]{1,0:T(8,128)(2,1)}, f32[512,256]{1,0:T(8,128)}) custom-call(bf16[32,2,16,256]{3,2,1,0:T(8,128)(2,1)} %copy-done.2, bf16[512,256]{1,0:T(8,128)(2,1)} %get-tuple-element.62.refs_1_, bf16[512,256]{1,0:T(8,128)(2,1)} %bitcast.17, bf16[512,256]{1,0:T(8,128)(2,1)} %refs_3_.3, bf16[512,256]{1,0:T(8,128)(2,1)} %refs_4_.3), custom_call_target="tpu_custom_call" | custom-call | flops 3000000000 | bytes 9000000 | tf_op jit(solution)/shard_map/post/pallas_call | solution.py:188
  116.5 2.6 %collective-permute-start.12 = (bf16[512,128]{1,0:T(8,128)(2,1)}, bf16[512,128]{1,0:T(8,128)(2,1)S(1)}, u32[]{:S(2)}, u32[]{:S(2)}) collective-permute-start(bf16[512,128]{1,0:T(8,128)(2,1)} %get-tuple-element.64), channel_id=1, source_target_pairs={{8,0},{16,8},{24,16},{32,24},{40,32},{48,40},{56,48},{64,56},{72,6... | collective-permute-start | bytes 393224 | tf_op jit(solution)/shard_map/ppermute | solution.py:454
  119.1 1.3 collective-permute-start.13
  120.4 1.1 collective-permute-start.14
  121.4 1.4 collective-permute-start.15
  122.8 7.9 %collective-permute-done.12.refs_1_ = bf16[512,128]{1,0:T(8,128)(2,1)S(1)} collective-permute-done((bf16[512,128]{1,0:T(8,128)(2,1)}, bf16[512,128]{1,0:T(8,128)(2,1)S(1)}, u32[]{:S(2)}, u32[]{:S(2)}) %collective-permute-start.12) | collective-permute-done | bytes 131104 | tf_op jit(solution)/shard_map/ppermute | solution.py:454
  130.7 0.6 copy-done.22
  131.3 6.7 %feature.1 = bf16[3,512,256]{2,1,0:T(8,128)(2,1)} custom-call(bf16[3,512,256]{2,1,0:T(8,128)(2,1)} %get-tuple-element.63.refs_0_, bf16[512,128]{1,0:T(8,128)(2,1)} %copy-done.22, f32[3,7,512]{2,1,0:T(8,128)} %bitcast.19), custom_call_target="tpu_custom_call" | custom-call | flops 3000000000 | bytes 9000000 | tf_op jit(solution)/shard_map/feature/pallas_call | solution.py:188
  138.1 0.0 collective-permute-done.14
  138.1 0.0 collective-permute-done.15
  138.1 0.8 add_add_fusion
  (35 shorter events, 0.1 us)
Async XLA Ops:
  0.6 12.6 %collective-permute-start.2 = (bf16[512,256]{1,0:T(8,128)(2,1)}, bf16[512,256]{1,0:T(8,128)(2,1)S(1)}, u32[]{:S(2)}, u32[]{:S(2)}) collective-permute-start(bf16[512,256]{1,0:T(8,128)(2,1)} %refs_0_.3), channel_id=1, source_target_pairs={{0,6},{1,7},{2,0},{3,1},{4,2},{5,3},{6,4},{7,5},{8,14},{9,15},{10,... | collective-permute-start | bytes 786440 | tf_op jit(solution)/shard_map/ppermute | solution.py:364
  3.4 9.8 %collective-permute-start.1 = (bf16[512,256]{1,0:T(8,128)(2,1)}, bf16[512,256]{1,0:T(8,128)(2,1)S(1)}, u32[]{:S(2)}, u32[]{:S(2)}) collective-permute-start(bf16[512,256]{1,0:T(8,128)(2,1)} %refs_0_.3), channel_id=1, source_target_pairs={{0,2},{1,3},{2,4},{3,5},{4,6},{5,7},{6,0},{7,1},{8,10},{9,11},{10,... | collective-permute-start | bytes 786440 | tf_op jit(solution)/shard_map/ppermute | solution.py:364
  3.4 17.6 %collective-permute-start = (bf16[512,256]{1,0:T(8,128)(2,1)}, bf16[512,256]{1,0:T(8,128)(2,1)S(1)}, u32[]{:S(2)}, u32[]{:S(2)}) collective-permute-start(bf16[512,256]{1,0:T(8,128)(2,1)} %refs_0_.3), channel_id=1, source_target_pairs={{0,1},{1,0},{2,3},{3,2},{4,5},{5,4},{6,7},{7,6},{8,9},{9,8},{10,11... | collective-permute-start | bytes 786440 | tf_op jit(solution)/shard_map/ppermute | solution.py:363
  9.5 11.6 %collective-permute-start.3 = (bf16[512,256]{1,0:T(8,128)(2,1)}, bf16[512,256]{1,0:T(8,128)(2,1)S(1)}, u32[]{:S(2)}, u32[]{:S(2)}) collective-permute-start(bf16[512,256]{1,0:T(8,128)(2,1)} %refs_0_.3), channel_id=1, source_target_pairs={{0,4},{1,5},{2,6},{3,7},{4,0},{5,1},{6,2},{7,3},{8,12},{9,13},{10,... | collective-permute-start | bytes 786440 | tf_op jit(solution)/shard_map/ppermute | solution.py:364
  13.2 22.3 %copy-start.11 = (bf16[512,256]{1,0:T(8,128)(2,1)}, bf16[512,256]{1,0:T(8,128)(2,1)S(1)}, u32[]{:S(2)}) copy-start(bf16[512,256]{1,0:T(8,128)(2,1)S(1)} %collective-permute-done.2.refs_3_) | copy-start | bytes 786436
  13.2 22.3 %copy-start.12 = (bf16[512,256]{1,0:T(8,128)(2,1)}, bf16[512,256]{1,0:T(8,128)(2,1)S(1)}, u32[]{:S(2)}) copy-start(bf16[512,256]{1,0:T(8,128)(2,1)S(1)} %collective-permute-done.1.refs_2_) | copy-start | bytes 786436
  21.1 17.8 %copy-start.13 = (bf16[512,256]{1,0:T(8,128)(2,1)}, bf16[512,256]{1,0:T(8,128)(2,1)S(1)}, u32[]{:S(2)}) copy-start(bf16[512,256]{1,0:T(8,128)(2,1)S(1)} %collective-permute-done.refs_1_) | copy-start | bytes 786436
  21.1 14.5 %copy-start.14 = (bf16[512,256]{1,0:T(8,128)(2,1)}, bf16[512,256]{1,0:T(8,128)(2,1)S(1)}, u32[]{:S(2)}) copy-start(bf16[512,256]{1,0:T(8,128)(2,1)S(1)} %collective-permute-done.3.refs_4_) | copy-start | bytes 786436
  21.1 21.1 %all-to-all-start = ((bf16[32,2,16,256]{3,2,1,0:T(8,128)(2,1)}), bf16[32,2,16,256]{3,2,1,0:T(8,128)(2,1)S(1)}, u32[]{:S(2)}, u32[]{:S(2)}) async-start(bf16[32,2,16,256]{3,2,1,0:T(8,128)(2,1)} %prep.1), calls=%async_computation | async-start | bytes 1048576 | tf_op jit(solution)/shard_map/all_to_all | solution.py:354
  36.2 19.1 %collective-permute-start.6 = (bf16[512,256]{1,0:T(8,128)(2,1)S(1)}, bf16[512,256]{1,0:T(8,128)(2,1)S(1)}, u32[]{:S(2)}, u32[]{:S(2)}) collective-permute-start(bf16[512,256]{1,0:T(8,128)(2,1)S(1)} %collective-permute-done.refs_1_), channel_id=1, source_target_pairs={{0,4},{1,5},{2,6},{3,7},{4,0},{5,1},{6,2},{7,3},{8,12},{9,13},{10,... | collective-permute-start | bytes 786440 | tf_op jit(solution)/shard_map/ppermute | solution.py:370
  37.8 17.5 %collective-permute-start.5 = (bf16[512,256]{1,0:T(8,128)(2,1)S(1)}, bf16[512,256]{1,0:T(8,128)(2,1)S(1)}, u32[]{:S(2)}, u32[]{:S(2)}) collective-permute-start(bf16[512,256]{1,0:T(8,128)(2,1)S(1)} %collective-permute-done.refs_1_), channel_id=1, source_target_pairs={{0,6},{1,7},{2,0},{3,1},{4,2},{5,3},{6,4},{7,5},{8,14},{9,15},{10,... | collective-permute-start | bytes 786440 | tf_op jit(solution)/shard_map/ppermute | solution.py:370
  38.9 16.5 %collective-permute-start.4 = (bf16[512,256]{1,0:T(8,128)(2,1)S(1)}, bf16[512,256]{1,0:T(8,128)(2,1)S(1)}, u32[]{:S(2)}, u32[]{:S(2)}) collective-permute-start(bf16[512,256]{1,0:T(8,128)(2,1)S(1)} %collective-permute-done.refs_1_), channel_id=1, source_target_pairs={{0,2},{1,3},{2,4},{3,5},{4,6},{5,7},{6,0},{7,1},{8,10},{9,11},{10,... | collective-permute-start | bytes 786440 | tf_op jit(solution)/shard_map/ppermute | solution.py:370
  42.1 0.8 copy-start.1
  47.9 15.6 %all-to-all-start.1 = ((bf16[32,16,256]{2,1,0:T(8,128)(2,1)}), bf16[32,16,256]{2,1,0:T(8,128)(2,1)S(1)}, u32[]{:S(2)}, u32[]{:S(2)}) async-start(bf16[32,16,256]{2,1,0:T(8,128)(2,1)} %get-tuple-element.39), calls=%async_computation.1 | async-start | bytes 524288 | tf_op jit(solution)/shard_map/all_to_all | solution.py:354
  55.3 0.7 copy-start.16
  55.3 0.8 copy-start.17
  55.3 0.8 copy-start.18
  56.2 8.1 %copy-start.3 = (bf16[512,256]{1,0:T(8,128)(2,1)S(1)}, bf16[512,256]{1,0:T(8,128)(2,1)}, u32[]{:S(2)}) copy-start(bf16[512,256]{1,0:T(8,128)(2,1)} %query_hbm.1) | copy-start | bytes 786436
  63.5 13.7 %copy-start = (bf16[32,16,256]{2,1,0:T(8,128)(2,1)}, bf16[32,16,256]{2,1,0:T(8,128)(2,1)S(1)}, u32[]{:S(2)}) copy-start(bf16[32,16,256]{2,1,0:T(8,128)(2,1)S(1)} %all-to-all-done.1) | copy-start | bytes 786436
  63.5 8.2 %collective-permute-start.7 = (bf16[16,128,256]{2,1,0:T(8,128)(2,1)}, bf16[16,128,256]{2,1,0:T(8,128)(2,1)S(1)}, u32[]{:S(2)}, u32[]{:S(2)}) collective-permute-start(bf16[16,128,256]{2,1,0:T(8,128)(2,1)} %get-tuple-element.49), channel_id=1, source_target_pairs={{0,8},{8,0},{16,24},{24,16},{32,40},{40,32},{48,56},{56,48},{64,72... | collective-permute-start | bytes 3145736 | tf_op jit(solution)/shard_map/ppermute | solution.py:396
  64.4 7.3 %copy-start.4 = (bf16[512,256]{1,0:T(8,128)(2,1)}, bf16[512,256]{1,0:T(8,128)(2,1)S(1)}, u32[]{:S(2)}) copy-start(bf16[512,256]{1,0:T(8,128)(2,1)S(1)} %multiply_convert_fusion.refs_3_) | copy-start | bytes 786436
  64.4 7.3 %collective-permute-start.8 = (bf16[512,256]{1,0:T(8,128)(2,1)S(1)}, bf16[512,256]{1,0:T(8,128)(2,1)S(1)}, u32[]{:S(2)}, u32[]{:S(2)}) collective-permute-start(bf16[512,256]{1,0:T(8,128)(2,1)S(1)} %multiply_convert_fusion.refs_3_), channel_id=1, source_target_pairs={{0,8},{8,0},{16,24},{24,16},{32,40},{40,32},{48,56},{56,48},{64,72... | collective-permute-start | bytes 786440 | tf_op jit(solution)/shard_map/ppermute | solution.py:398
  64.5 15.2 %all-to-all-start.2 = ((bf16[32,16,256]{2,1,0:T(8,128)(2,1)}), bf16[32,16,256]{2,1,0:T(8,128)(2,1)S(1)}, u32[]{:S(2)}, u32[]{:S(2)}) async-start(bf16[32,16,256]{2,1,0:T(8,128)(2,1)} %bitcast.18), calls=%async_computation.2 | async-start | bytes 524288 | tf_op jit(solution)/shard_map/all_to_all | solution.py:354
  71.6 0.7 copy-start.15
  71.6 1.1 copy-start.7
  77.2 17.8 %collective-permute-start.9 = (bf16[4,128,512]{2,1,0:T(8,128)(2,1)}, bf16[4,128,512]{2,1,0:T(8,128)(2,1)S(1)}, u32[]{:S(2)}, u32[]{:S(2)}) collective-permute-start(bf16[4,128,512]{2,1,0:T(8,128)(2,1)} %get-tuple-element.56), channel_id=1, source_target_pairs={{0,16},{8,24},{16,32},{24,40},{32,48},{40,56},{48,0},{56,8},{64,80... | collective-permute-start | bytes 1572872 | tf_op jit(solution)/shard_map/ppermute | solution.py:413
  77.5 17.5 %collective-permute-start.10 = (bf16[4,128,512]{2,1,0:T(8,128)(2,1)}, bf16[4,128,512]{2,1,0:T(8,128)(2,1)S(1)}, u32[]{:S(2)}, u32[]{:S(2)}) collective-permute-start(bf16[4,128,512]{2,1,0:T(8,128)(2,1)} %get-tuple-element.57), channel_id=1, source_target_pairs={{0,32},{8,40},{16,48},{24,56},{32,0},{40,8},{48,16},{56,24},{64,96... | collective-permute-start | bytes 1572872 | tf_op jit(solution)/shard_map/ppermute | solution.py:413
  79.6 29.2 %collective-permute-start.11 = (bf16[4,128,512]{2,1,0:T(8,128)(2,1)}, bf16[4,128,512]{2,1,0:T(8,128)(2,1)S(1)}, u32[]{:S(2)}, u32[]{:S(2)}) collective-permute-start(bf16[4,128,512]{2,1,0:T(8,128)(2,1)} %get-tuple-element.58), channel_id=1, source_target_pairs={{0,48},{8,56},{16,0},{24,8},{32,16},{40,24},{48,32},{56,40},{64,11... | collective-permute-start | bytes 1572872 | tf_op jit(solution)/shard_map/ppermute | solution.py:413
  79.6 0.7 copy-start.6
  86.4 26.5 %all-to-all-start.3 = ((bf16[32,2,16,256]{3,2,1,0:T(8,128)(2,1)}), bf16[32,2,16,256]{3,2,1,0:T(8,128)(2,1)S(1)}, u32[]{:S(2)}, u32[]{:S(2)}) async-start(bf16[32,2,16,256]{3,2,1,0:T(8,128)(2,1)} %grad.1), calls=%async_computation.3 | async-start | bytes 1048576 | tf_op jit(solution)/shard_map/all_to_all | solution.py:354
  95.0 13.8 %copy-start.8 = (bf16[4,128,512]{2,1,0:T(8,128)(2,1)}, bf16[4,128,512]{2,1,0:T(8,128)(2,1)S(1)}, u32[]{:S(2)}) copy-start(bf16[4,128,512]{2,1,0:T(8,128)(2,1)S(1)} %collective-permute-done.9.refs_2_) | copy-start | bytes 1572868
  95.0 13.8 %copy-start.9 = (bf16[4,128,512]{2,1,0:T(8,128)(2,1)}, bf16[4,128,512]{2,1,0:T(8,128)(2,1)S(1)}, u32[]{:S(2)}) copy-start(bf16[4,128,512]{2,1,0:T(8,128)(2,1)S(1)} %collective-permute-done.10.refs_3_) | copy-start | bytes 1572868
  108.8 0.8 copy-start.10
  112.9 0.8 copy-start.2
  113.7 5.3 %copy-start.21 = (bf16[128,512]{1,0:T(8,128)(2,1)S(1)}, bf16[128,512]{1,0:T(8,128)(2,1)}, u32[]{:S(2)}) copy-start(bf16[128,512]{1,0:T(8,128)(2,1)} %get-tuple-element.68) | copy-start | bytes 393220
  113.7 6.6 %copy-start.20 = (bf16[128,512]{1,0:T(8,128)(2,1)S(1)}, bf16[128,512]{1,0:T(8,128)(2,1)}, u32[]{:S(2)}) copy-start(bf16[128,512]{1,0:T(8,128)(2,1)} %get-tuple-element.69) | copy-start | bytes 393220
  113.7 7.7 %copy-start.19 = (bf16[128,512]{1,0:T(8,128)(2,1)S(1)}, bf16[128,512]{1,0:T(8,128)(2,1)}, u32[]{:S(2)}) copy-start(bf16[128,512]{1,0:T(8,128)(2,1)} %get-tuple-element.70) | copy-start | bytes 393220
  116.5 14.2 %collective-permute-start.12 = (bf16[512,128]{1,0:T(8,128)(2,1)}, bf16[512,128]{1,0:T(8,128)(2,1)S(1)}, u32[]{:S(2)}, u32[]{:S(2)}) collective-permute-start(bf16[512,128]{1,0:T(8,128)(2,1)} %get-tuple-element.64), channel_id=1, source_target_pairs={{8,0},{16,8},{24,16},{32,24},{40,32},{48,40},{56,48},{64,56},{72,6... | collective-permute-start | bytes 393224 | tf_op jit(solution)/shard_map/ppermute | solution.py:454
  119.1 19.0 %collective-permute-start.13 = (bf16[128,512]{1,0:T(8,128)(2,1)S(1)}, bf16[128,512]{1,0:T(8,128)(2,1)S(1)}, u32[]{:S(2)}, u32[]{:S(2)}) collective-permute-start(bf16[128,512]{1,0:T(8,128)(2,1)S(1)} %copy-done.21), channel_id=1, source_target_pairs={{0,64},{8,72},{16,80},{24,88},{32,96},{40,104},{48,112},{56,120},{... | collective-permute-start | bytes 393224 | tf_op jit(solution)/shard_map/ppermute | solution.py:441
  120.4 17.7 %collective-permute-start.14 = (bf16[128,512]{1,0:T(8,128)(2,1)S(1)}, bf16[128,512]{1,0:T(8,128)(2,1)S(1)}, u32[]{:S(2)}, u32[]{:S(2)}) collective-permute-start(bf16[128,512]{1,0:T(8,128)(2,1)S(1)} %copy-done.20), channel_id=1, source_target_pairs={{0,128},{8,136},{16,144},{24,152},{32,160},{40,168},{48,176},{56,1... | collective-permute-start | bytes 393224 | tf_op jit(solution)/shard_map/ppermute | solution.py:441
  121.4 16.6 %collective-permute-start.15 = (bf16[128,512]{1,0:T(8,128)(2,1)S(1)}, bf16[128,512]{1,0:T(8,128)(2,1)S(1)}, u32[]{:S(2)}, u32[]{:S(2)}) collective-permute-start(bf16[128,512]{1,0:T(8,128)(2,1)S(1)} %copy-done.19), channel_id=1, source_target_pairs={{0,192},{8,200},{16,208},{24,216},{32,224},{40,232},{48,240},{56,2... | collective-permute-start | bytes 393224 | tf_op jit(solution)/shard_map/ppermute | solution.py:441
  130.7 0.6 copy-start.22
  131.3 6.7 %copy-start.5 = (f32[128,512]{1,0:T(8,128)S(1)}, f32[128,512]{1,0:T(8,128)}, u32[]{:S(2)}) copy-start(f32[128,512]{1,0:T(8,128)} %get-tuple-element.67) | copy-start | bytes 786436
